TPU v7x, 32 devices: a whole 2x2x4 slice. The times are simulated.
32 devices in a mesh: dom: 8 (over z, y), cls: 4 (over x, core).
Axes of the slice: x: 2, y: 2, z: 4, core: 2. Of those that a mesh axis runs over, the one named last changes fastest.
Arguments:
- particles: bfloat16 [512, 2, 36, 128], P('dom'), may hold values from -16 to 16
- references: bfloat16 [48, 2, 36, 128], P('cls', None, None, 'dom'), may hold values from -8 to 8
- noise_weights: float32 [128], replicated, may hold values from 0.005 to 0.2
Outputs:
- class_spectra: float32 [48, 2, 36, 128], P('cls', None, None, 'dom')
- log_evidence: float32 [512], P('dom')
All inputs are finite; a program needn't handle non-finite values.
Results may differ from a plain program's by a relative error of at most 0.035.
Values may be sent and summed in bfloat16 or wider, within the bound.
A program may use at most 64 MiB of HBM per device.

v0:
```python
import jax
import jax.numpy as jnp
from jax import lax
from jax.sharding import PartitionSpec as P

SHIFTS = 5


ridge_term = 0.5
shift_x = (0.0, 1.0, -1.0, 0.0, 0.0)
shift_y = (0.0, 0.0, 0.0, 1.0, -1.0)


def phase_tables(angles, cycles, shift_index):
    theta = 2.0 * jnp.pi * jnp.arange(angles, dtype=jnp.float32) / angles
    radius = jnp.arange(cycles, dtype=jnp.float32) / (2.0 * cycles)
    along = shift_x[shift_index] * jnp.cos(theta) + shift_y[shift_index] * jnp.sin(theta)
    phase = -2.0 * jnp.pi * along[:, None] * radius[None, :]
    return (jnp.cos(phase), jnp.sin(phase))


def rotation_tables(angles):
    steps = jnp.arange(angles, dtype=jnp.int32)
    product = steps[:, None] * steps[None, :] % angles
    turn = 2.0 * jnp.pi * product.astype(jnp.float32) / angles
    return (jnp.cos(turn), jnp.sin(turn))


def angular_table(angles):
    cosine, sine = rotation_tables(angles)
    upper = jnp.stack([cosine, -sine], axis=1)
    lower = jnp.stack([sine, cosine], axis=1)
    return jnp.stack([upper, lower], axis=0).astype(jnp.bfloat16)


def shifted_spectra(block, shift_index, table):
    cosine, sine = phase_tables(block.shape[2], block.shape[3], shift_index)
    real_part = block[:, 0].astype(jnp.float32)
    imag_part = block[:, 1].astype(jnp.float32)
    shifted = jnp.stack(
        [real_part * cosine - imag_part * sine, real_part * sine + imag_part * cosine], axis=1
    )
    shifted = shifted.astype(jnp.bfloat16)
    spectra = jnp.einsum("npar,paqm->nqmr", shifted, table, preferred_element_type=jnp.float32)
    return spectra.astype(jnp.bfloat16)


def per_device(particles, references, noise_weights):
    angles = particles.shape[2]
    cycles = particles.shape[3]
    table = angular_table(angles)
    cosine_k, sine_k = rotation_tables(angles)
    whole = lax.all_gather(references, "dom", axis=3, tiled=True)
    ref_spectra = jnp.einsum("cpar,paqm->cqmr", whole, table, preferred_element_type=jnp.float32)
    weighted = (noise_weights * ref_spectra).astype(jnp.bfloat16)
    whole_wide = whole.astype(jnp.float32)
    class_norms = jnp.sum(noise_weights * whole_wide * whole_wide, axis=(1, 2, 3))
    stacked = jnp.concatenate(
        [weighted, jnp.stack([-weighted[:, 1], weighted[:, 0]], axis=1)], axis=0
    )
    classes = class_norms.shape[0]
    score_list = []
    for shift_index in range(SHIFTS):
        spectra = shifted_spectra(particles, shift_index, table)
        correlation = jnp.einsum(
            "nqmr,dqmr->mnd", spectra, stacked, preferred_element_type=jnp.float32
        )
        real_correlation = correlation[:, :, :classes]
        imag_correlation = correlation[:, :, classes:]
        score = (
            jnp.einsum("mnc,mk->nck", real_correlation, cosine_k, precision=lax.Precision.HIGHEST)
            - jnp.einsum("mnc,mk->nck", imag_correlation, sine_k, precision=lax.Precision.HIGHEST)
        ) / angles
        score_list.append(score - 0.5 * class_norms[None, :, None])
    scores = jnp.stack(score_list, axis=2)
    local_peaks = jnp.max(scores, axis=(1, 2, 3))
    peaks = lax.pmax(local_peaks, "cls")
    expo = jnp.exp(scores - peaks[:, None, None, None])
    totals = lax.psum(jnp.sum(expo, axis=(1, 2, 3)), "cls")
    posterior = expo / totals[:, None, None, None]
    evidence = peaks + jnp.log(totals)
    sums = jnp.zeros((classes, 2, angles, cycles), jnp.float32)
    for shift_index in range(SHIFTS):
        spectra = shifted_spectra(particles, shift_index, table)
        chosen = posterior[:, :, shift_index, :]
        real_weight = jnp.einsum("nck,mk->ncm", chosen, cosine_k, precision=lax.Precision.HIGHEST)
        imag_weight = jnp.einsum("nck,mk->ncm", chosen, sine_k, precision=lax.Precision.HIGHEST)
        both = jnp.stack([real_weight, imag_weight], axis=1).astype(jnp.bfloat16)
        parts = jnp.einsum("npcm,nqmr->pqcmr", both, spectra, preferred_element_type=jnp.float32)
        real_sum = parts[0, 0] - parts[1, 1]
        imag_sum = parts[0, 1] + parts[1, 0]
        sums = sums + jnp.stack([real_sum, imag_sum], axis=1)
    weight_sums = jnp.sum(posterior, axis=(0, 2, 3))
    denominator = (noise_weights[None, :] * weight_sums[:, None])[:, None, None, :]
    cycle_count = cycles // lax.axis_size("dom")
    cycle_start = lax.axis_index("dom") * cycle_count
    own_sums, own_denominator = (
        lax.psum_scatter(sums.astype(jnp.bfloat16), "dom", scatter_dimension=3, tiled=True).astype(
            jnp.float32
        ),
        lax.psum_scatter(
            denominator.astype(jnp.bfloat16), "dom", scatter_dimension=3, tiled=True
        ).astype(jnp.float32),
    )
    own_weights = lax.dynamic_slice_in_dim(noise_weights, cycle_start, cycle_count, 0)
    class_spectra = own_weights * own_sums / (own_denominator + ridge_term)
    return (class_spectra, evidence)


def solution(mesh):
    return jax.shard_map(
        per_device,
        mesh=mesh,
        in_specs=(P("dom", None, None, None), P("cls", None, None, "dom"), P()),
        out_specs=(P("cls", None, None, "dom"), P("dom")),
        check_vma=False,
    )
```

profile of v0, /device:TPU:0, one launch (start us, length us, event | category | flops | bytes accessed | tf_op | source)
XLA Modules:
  0.0 216.6 jit_solution(6904572420411022669)
XLA Ops:
  7.6 3.7 %fusion.290 = (bf16[64,1,36,128]{3,1,2,0:T(2,128)(2,1)S(1)}, bf16[64,1,36,128]{3,1,2,0:T(2,128)(2,1)S(1)}) fusion(bf16[64,2,36,128]{3,1,2,0:T(2,128)(2,1)} %param.3), kind=kLoop, calls=%fused_computation.372 | loop fusion | bytes 2359296 | tf_op jit(solution)/shard_map/slice | solution.py:38
  11.4 33.9 %all_gather.3 = bf16[12,2,36,128]{2,3,1,0:T(8,128)(2,1)S(1)} all-gather(bf16[12,2,36,16]{2,3,1,0:T(8,128)(2,1)S(1)} %copy-done.10), channel_id=1, replica_groups=mesh['dom'=8,'cls'=4] {'dom'}, dimensions={3}, use_global_device_ids=true | all-gather | bytes 248832 | tf_op jit(solution)/shard_map/all_gather | solution.py:53
  47.0 1.7 fusion.14
  48.7 0.6 bitcast_convert_fusion.4
  49.8 0.6 copy-done.8
  50.9 0.6 bitcast_convert_fusion.3
  52.0 0.6 copy-done
  54.1 0.6 copy-done.2
  55.2 0.6 bitcast_convert_fusion.1
  56.2 0.6 copy-done.4
  58.4 0.6 copy-done.6
  62.5 5.9 %pmax.7 = f32[64]{0:T(128)S(1)} all-reduce(f32[64]{0:T(128)S(1)} %maximum_maximum_fusion.1), channel_id=1, replica_groups=mesh['dom'=8,'cls'=4] {'cls'}, use_global_device_ids=true, to_apply=%region_6.7 | all-reduce | flops 64 | bytes 512 | tf_op jit(solution)/shard_map/pmax | solution.py:77
  68.7 6.6 %psum.7 = f32[64]{0:T(128)S(1)} all-reduce(f32[64]{0:T(128)S(1)} %fusion.65), channel_id=1, replica_groups=mesh['dom'=8,'cls'=4] {'cls'}, use_global_device_ids=true, to_apply=%region_8.9 | all-reduce | flops 64 | bytes 512 | tf_op jit(solution)/shard_map/psum | solution.py:79
  75.9 0.6 copy.253
  82.4 1.2 copy-done.3
  84.1 1.2 copy-done.5
  85.7 1.2 copy-done.7
  87.5 1.7 copy.104
  89.9 0.6 dynamic-slice
  91.1 39.6 %reduce-scatter.4.cloned.1.call-done = bf16[16,12]{1,0:T(8,128)(2,1)} async-done(((bf16[128,12]{1,0:T(8,128)(2,1)}), bf16[16,12]{1,0:T(8,128)(2,1)}) %reduce-scatter.4.cloned.1.call-update) | async-done | bytes 400
  130.7 0.7 reshape_bitcast_fusion
  131.5 76.3 %all-reduce.3.cloned.1.call-done = bf16[12,2,36,128]{2,1,0,3:T(2,128)(2,1)} async-done(((bf16[12,2,36,128]{2,1,0,3:T(2,128)(2,1)}), bf16[12,2,36,128]{2,1,0,3:T(2,128)(2,1)}) %all-reduce.3.cloned.1.call-update) | async-done | bytes 221200
  207.9 1.2 multiply_divide_fusion
  209.0 0.7 copy.106
  (100 shorter events, 20.0 us)
Async XLA Ops:
  7.2 123.5 %reduce-scatter.4.cloned.1.call-start = ((), (), s32[]{:S(2)}) async-start(), calls=%async_computation.1 | async-start | bytes 36864
  7.6 3.8 %copy-start.10 = (bf16[12,2,36,16]{2,3,1,0:T(8,128)(2,1)S(1)}, bf16[12,2,36,16]{2,3,1,0:T(8,128)(2,1)}, u32[]{:S(2)}) copy-start(bf16[12,2,36,16]{2,3,1,0:T(8,128)(2,1)} %param.4) | copy-start | bytes 82948
  7.6 37.7 %copy-start.11 = (f32[128]{0:T(128)S(1)}, f32[128]{0:T(128)}, u32[]{:S(2)}) copy-start(f32[128]{0:T(128)} %param.5) | copy-start | bytes 1540
  49.3 1.1 copy-start.8
  51.5 1.1 copy-start
  53.6 1.1 copy-start.2
  55.8 1.0 copy-start.4
  57.9 1.1 copy-start.6
  75.7 1.9 copy-start.9
  76.6 131.3 %all-reduce.3.cloned.1.call-start = ((), (), s32[]{:S(2)}) async-start(), calls=%async_computation.2 | async-start | bytes 1572864
  79.0 2.9 %copy-start.1 = (bf16[2,36,64,128]{3,1,2,0:T(8,128)(2,1)S(1)}, bf16[2,36,64,128]{3,1,2,0:T(8,128)(2,1)}, u32[]{:S(2)}) copy-start(bf16[2,36,64,128]{3,1,2,0:T(8,128)(2,1)} %copy-done) | copy-start | bytes 3538948
  82.3 1.3 copy-start.3
  83.9 1.3 copy-start.5
  85.5 1.3 copy-start.7
  87.5 2.4 %copy-start.12 = (u32[32]{0:T(128)S(1)}, u32[32]{0:T(128)}, u32[]{:S(2)}) copy-start(u32[32]{0:T(128)} %constant.59) | copy-start | bytes 388
Sparse Core Ops, SparseCore 0:
  76.7 53.9 reduce-scatter.3
  134.1 73.7 all-reduce.2
where the time goes:
time: 217 us
  waiting for transfers between devices  116 us (53%)
  blocking collectives  46.4 us (21%)
  matrix products  16.5 us (8%)
  local copies, waits for them, and re-layouts  15.2 us (7%)
  between operations  15.2 us (7%)
  other arithmetic  7.21 us (3%)
    unnamed x4, waiting for transfers between devices  116 us
    all_gather x1, blocking collectives, per_device(): whole = lax.all_gather(references, 'dom', axis=3, tiled=True)  33.9 us
    unnamed x32, local copies, waits for them, and re-layouts  9.31 us
    psum x1, blocking collectives, per_device(): totals = lax.psum(jnp.sum(expo, axis=(1, 2, 3)), 'cls')  6.61 us
    pmax x1, blocking collectives, per_device(): peaks = lax.pmax(local_peaks, 'cls')  5.88 us
  transfers between devices with their start and end apart: 2, of which 2 were waited for; matrix products, arithmetic and copies ran while one was open for 5% of the time, Pallas kernels for 0%

commit v1 on v0

v1 whole, which is shorter than its diff:
```python
import functools

import jax
import jax.numpy as jnp
from jax import lax
from jax.experimental import pallas as pl
from jax.experimental.pallas import tpu as pltpu
from jax.sharding import PartitionSpec as P

SHIFTS = 5
MESH = pl.DeviceIdType.MESH

ridge_term = 0.5
shift_x = (0.0, 1.0, -1.0, 0.0, 0.0)
shift_y = (0.0, 0.0, 0.0, 1.0, -1.0)


def phase_tables(angles, cycles, shift_index):
    theta = 2.0 * jnp.pi * jnp.arange(angles, dtype=jnp.float32) / angles
    radius = jnp.arange(cycles, dtype=jnp.float32) / (2.0 * cycles)
    along = shift_x[shift_index] * jnp.cos(theta) + shift_y[shift_index] * jnp.sin(theta)
    phase = -2.0 * jnp.pi * along[:, None] * radius[None, :]
    return (jnp.cos(phase), jnp.sin(phase))


def rotation_tables(angles):
    steps = jnp.arange(angles, dtype=jnp.int32)
    product = steps[:, None] * steps[None, :] % angles
    turn = 2.0 * jnp.pi * product.astype(jnp.float32) / angles
    return (jnp.cos(turn), jnp.sin(turn))


def angular_table(angles):
    cosine, sine = rotation_tables(angles)
    upper = jnp.stack([cosine, -sine], axis=1)
    lower = jnp.stack([sine, cosine], axis=1)
    return jnp.stack([upper, lower], axis=0).astype(jnp.bfloat16)


def greet(axis, count):
    me = lax.axis_index(axis)
    barrier = pltpu.get_barrier_semaphore()
    for step in range(1, count):
        pl.semaphore_signal(
            barrier,
            inc=1,
            device_id={axis: lax.rem(me + step, count)},
            device_id_type=MESH,
        )
    pl.semaphore_wait(barrier, count - 1)
    return me


def push(axis, count, me, source, land, send_sem, recv_sem):
    copies = []
    for step in range(1, count):
        peer = lax.rem(me + step, count)
        copy = pltpu.make_async_remote_copy(
            src_ref=source(peer),
            dst_ref=land.at[me],
            send_sem=send_sem.at[step],
            recv_sem=recv_sem.at[step],
            device_id={axis: peer},
            device_id_type=MESH,
        )
        copy.start()
        copies.append(copy)
    return copies


def gather_kernel(axis, count, x_ref, o_ref, land, send_sem, recv_sem):
    me = greet(axis, count)
    copies = push(axis, count, me, lambda peer: x_ref, land, send_sem, recv_sem)
    land[me] = x_ref[...]
    for copy in copies:
        copy.wait()
    o_ref[...] = land[...]


def gather(axis, count, identity, x):
    return pl.pallas_call(
        functools.partial(gather_kernel, axis, count),
        out_shape=jax.ShapeDtypeStruct((count,) + x.shape, x.dtype),
        in_specs=[pl.BlockSpec(memory_space=pltpu.VMEM)],
        out_specs=pl.BlockSpec(memory_space=pltpu.VMEM),
        scratch_shapes=[
            pltpu.VMEM((count,) + x.shape, x.dtype),
            pltpu.SemaphoreType.DMA((count,)),
            pltpu.SemaphoreType.DMA((count,)),
        ],
        compiler_params=pltpu.CompilerParams(collective_id=identity, has_side_effects=True),
    )(x)


def scatter_kernel(
    axis, count, x_ref, t_ref, o_ref, u_ref, land, t_land, send_sem, recv_sem, t_send, t_recv
):
    me = greet(axis, count)
    copies = push(axis, count, me, lambda peer: x_ref.at[peer], land, send_sem, recv_sem)
    copies += push(axis, count, me, lambda peer: t_ref, t_land, t_send, t_recv)
    land[me] = x_ref[me]
    t_land[me] = t_ref[...]
    for copy in copies:
        copy.wait()
    total = land[0].astype(jnp.float32)
    weight = t_land[0]
    for index in range(1, count):
        total = total + land[index].astype(jnp.float32)
        weight = weight + t_land[index]
    o_ref[...] = total
    u_ref[...] = weight


def scatter(axis, count, identity, x, t):
    return pl.pallas_call(
        functools.partial(scatter_kernel, axis, count),
        out_shape=(
            jax.ShapeDtypeStruct(x.shape[1:], jnp.float32),
            jax.ShapeDtypeStruct(t.shape, jnp.float32),
        ),
        in_specs=[pl.BlockSpec(memory_space=pltpu.VMEM)] * 2,
        out_specs=(pl.BlockSpec(memory_space=pltpu.VMEM),) * 2,
        scratch_shapes=[
            pltpu.VMEM(x.shape, x.dtype),
            pltpu.VMEM((count,) + t.shape, t.dtype),
            pltpu.SemaphoreType.DMA((count,)),
            pltpu.SemaphoreType.DMA((count,)),
            pltpu.SemaphoreType.DMA((count,)),
            pltpu.SemaphoreType.DMA((count,)),
        ],
        compiler_params=pltpu.CompilerParams(collective_id=identity, has_side_effects=True),
    )(x, t)


def posterior_kernel(axis, count, x_ref, o_ref, e_ref, mine, land, send_sem, recv_sem):
    me = greet(axis, count)
    peak = jnp.max(x_ref[...], axis=1, keepdims=True)
    expo = jnp.exp(x_ref[...] - peak)
    o_ref[...] = expo
    total = jnp.sum(expo, axis=1, keepdims=True)
    lanes = lax.broadcasted_iota(jnp.int32, mine.shape, 1)
    mine[...] = jnp.where(lanes == 0, peak, total)
    copies = push(axis, count, me, lambda peer: mine, land, send_sem, recv_sem)
    land[me] = mine[...]
    for copy in copies:
        copy.wait()
    peaks = land[0][:, 0:1]
    for index in range(1, count):
        peaks = jnp.maximum(peaks, land[index][:, 0:1])
    totals = jnp.zeros_like(peaks)
    for index in range(count):
        part = land[index]
        totals = totals + part[:, 1:2] * jnp.exp(part[:, 0:1] - peaks)
    o_ref[...] = o_ref[...] * (jnp.exp(peak - peaks) / totals)
    e_ref[...] = jnp.broadcast_to(peaks + jnp.log(totals), e_ref.shape)


def posteriors(axis, count, identity, x):
    rows = x.shape[0]
    return pl.pallas_call(
        functools.partial(posterior_kernel, axis, count),
        out_shape=(
            jax.ShapeDtypeStruct(x.shape, jnp.float32),
            jax.ShapeDtypeStruct((rows, 128), jnp.float32),
        ),
        in_specs=[pl.BlockSpec(memory_space=pltpu.VMEM)],
        out_specs=(pl.BlockSpec(memory_space=pltpu.VMEM),) * 2,
        scratch_shapes=[
            pltpu.VMEM((rows, 128), jnp.float32),
            pltpu.VMEM((count, rows, 128), jnp.float32),
            pltpu.SemaphoreType.DMA((count,)),
            pltpu.SemaphoreType.DMA((count,)),
        ],
        compiler_params=pltpu.CompilerParams(collective_id=identity, has_side_effects=True),
    )(x)


def per_device(dom, cls, particles, references, noise_weights):
    particle_count, _, angles, cycles = particles.shape
    classes = references.shape[0]
    cycle_count = cycles // dom
    rows = -(-cycle_count // 16) * 16
    wide = classes * 2 * angles
    table = angular_table(angles)
    cosine_k, sine_k = rotation_tables(angles)

    own = references.reshape(wide, cycle_count).T
    own = jnp.pad(own, ((0, rows - cycle_count), (0, 0)))
    whole = gather("dom", dom, 0, own)[:, :cycle_count].reshape(cycles, classes, 2, angles)
    whole_wide = whole.astype(jnp.float32)
    ref_spectra = jnp.einsum("rcpa,paqm->mqrc", whole, table, preferred_element_type=jnp.float32)
    weighted = (noise_weights[None, None, :, None] * ref_spectra).astype(jnp.bfloat16)
    class_norms = jnp.sum(noise_weights[:, None, None, None] * whole_wide * whole_wide, axis=(0, 2, 3))
    stacked = jnp.concatenate(
        [weighted, jnp.stack([-weighted[:, 1], weighted[:, 0]], axis=1)], axis=3
    )

    spectra_list = []
    for shift_index in range(SHIFTS):
        cosine, sine = phase_tables(angles, cycles, shift_index)
        real_part = particles[:, 0].astype(jnp.float32)
        imag_part = particles[:, 1].astype(jnp.float32)
        shifted = jnp.stack(
            [real_part * cosine - imag_part * sine, real_part * sine + imag_part * cosine], axis=1
        ).astype(jnp.bfloat16)
        spectra_list.append(
            jnp.einsum(
                "npar,paqm->mnqr", shifted, table, preferred_element_type=jnp.float32
            ).astype(jnp.bfloat16)
        )
    spectra = jnp.stack(spectra_list, axis=1)
    correlation = jnp.einsum("msnqr,mqrd->snmd", spectra, stacked, preferred_element_type=jnp.float32)
    turn = jnp.stack([cosine_k, -sine_k], axis=1) / angles
    both_parts = correlation.reshape(SHIFTS, particle_count, angles, 2, classes)
    scores = jnp.einsum("snmpc,mpk->nsck", both_parts, turn, precision=lax.Precision.HIGHEST)
    scores = scores - 0.5 * class_norms[None, None, :, None]
    posterior, evidence = posteriors("cls", cls, 1, scores.reshape(particle_count, -1))
    posterior = posterior.reshape(particle_count, SHIFTS, classes, angles)

    back = jnp.stack([cosine_k, sine_k], axis=0)
    both = jnp.einsum(
        "nsck,pmk->mpcsn", posterior, back, precision=lax.Precision.HIGHEST
    ).astype(jnp.bfloat16)
    parts = jnp.einsum("mpcsn,msnqr->mpcqr", both, spectra, preferred_element_type=jnp.float32)
    real_sum = parts[:, 0, :, 0] - parts[:, 1, :, 1]
    imag_sum = parts[:, 0, :, 1] + parts[:, 1, :, 0]
    sums = jnp.stack([real_sum, imag_sum], axis=2).astype(jnp.bfloat16)
    sums = jnp.transpose(sums, (3, 1, 2, 0)).reshape(dom, cycle_count, wide)
    sums = jnp.pad(sums, ((0, 0), (0, rows - cycle_count), (0, 0)))
    weight_sums = jnp.sum(posterior, axis=(0, 1, 3))
    weight_block = jnp.broadcast_to(weight_sums[None, :], (8, classes))
    own_sums, own_weights = scatter("dom", dom, 2, sums, weight_block)
    own_sums = own_sums[:cycle_count].T.reshape(classes, 2, angles, cycle_count)
    cycle_start = lax.axis_index("dom") * cycle_count
    noise = lax.dynamic_slice_in_dim(noise_weights, cycle_start, cycle_count, 0)
    denominator = noise * own_weights[0][:, None] + ridge_term
    class_spectra = own_sums * (noise / denominator)[:, None, None, :]
    return (class_spectra, evidence[:, 0])


def solution(mesh):
    dom, cls = mesh.shape["dom"], mesh.shape["cls"]
    return jax.shard_map(
        functools.partial(per_device, dom, cls),
        mesh=mesh,
        in_specs=(P("dom", None, None, None), P("cls", None, None, "dom"), P()),
        out_specs=(P("cls", None, None, "dom"), P("dom")),
        check_vma=False,
    )
```

time: 217 us -> 77.9 us (0.36)
  waiting for transfers between devices: 116 us -> 0 us
  blocking collectives: 46.4 us -> 0 us
  Pallas kernels: 0 us -> 31.9 us
  between operations: 15.2 us -> 0.89 us
  matrix products: 16.5 us -> 22.1 us
  other arithmetic: 7.21 us -> 4.71 us
  local copies, waits for them, and re-layouts: 15.2 us -> 17.7 us
    unnamed x4 -> x0, waiting for transfers between devices: 116 us -> none
    all_gather x1 -> x0, blocking collectives: 33.9 us -> none  [per_device(): whole = lax.all_gather(references, 'dom', axis=3, tiled=True)]
    pallas_call x0 -> x3, Pallas kernels: none -> 31.9 us  [the longest x1 13.6 us: scatter(): pl.pallas_call(functools.partial(scatter_kernel, axis, count), out_shape=...]
    unnamed x32 -> x11, local copies, waits for them, and re-layouts: 9.31 us -> 0.53 us
    reshape x0 -> x8, local copies, waits for them, and re-layouts: none -> 8.18 us  [the longest x2 2.58 us: per_device(): gather('dom', dom, 0, own)[:, :cycle_count]]
    psum x1 -> x0, blocking collectives: 6.61 us -> none  [per_device(): totals = lax.psum(jnp.sum(expo, axis=(1, 2, 3)), 'cls')]
    pmax x1 -> x0, blocking collectives: 5.88 us -> none  [per_device(): peaks = lax.pmax(local_peaks, 'cls')]
    dot_general x36 -> x10, matrix products: 16.5 us -> 22.1 us  [the longest x5 8.26 us: per_device(): jnp.einsum('npar,paqm->mnqr', shifted, table, preferred_element_type=jnp....]
  transfers between devices with their start and end apart: 2 -> 0, of which waited for: 2 -> 0; matrix products, arithmetic and copies ran while one was open for 5% -> 0% of each run, Pallas kernels for 0% -> 0%
where the time goes in v1:
time: 77.9 us; the launch traced here: 77.3 us
  Pallas kernels  31.9 us (41%)
  matrix products  22.1 us (28%)
  local copies, waits for them, and re-layouts  17.7 us (23%)
  other arithmetic  4.71 us (6%)
  between operations  0.89 us (1%)
    pallas_call x1, Pallas kernels, scatter(): pl.pallas_call(functools.partial(scatter_kernel, axis, count), out_shape=...  13.6 us
    pallas_call x1, Pallas kernels, gather(): pl.pallas_call(functools.partial(gather_kernel, axis, count), out_shape=j...  11.7 us
    dot_general x5, matrix products, per_device(): jnp.einsum('npar,paqm->mnqr', shifted, table, preferred_element_type=jnp....  8.26 us
    pallas_call x1, Pallas kernels, posteriors(): pl.pallas_call(functools.partial(posterior_kernel, axis, count), out_shap...  6.55 us
    dot_general x1, matrix products, per_device(): jnp.einsum('msnqr,mqrd->snmd', spectra, stacked, preferred_element_type=j...  5.12 us
    dot_general x1, matrix products, per_device(): jnp.einsum('mpcsn,msnqr->mpcqr', both, spectra, preferred_element_type=jn...  4.02 us
    slice x1, local copies, waits for them, and re-layouts, per_device(): real_part = particles[:, 0].astype(jnp.float32)  3.74 us
    reshape x2, local copies, waits for them, and re-layouts, per_device(): gather('dom', dom, 0, own)[:, :cycle_count]  2.58 us

profile of v1, /device:TPU:0, one launch (start us, length us, event | category | flops | bytes accessed | tf_op | source)
XLA Modules:
  0.0 77.3 jit_solution(16932903089452442428)
XLA Ops:
  1.2 3.7 %fusion.101 = (bf16[64,1,36,128]{3,1,2,0:T(2,128)(2,1)S(1)}, bf16[64,1,36,128]{3,1,2,0:T(2,128)(2,1)S(1)}) fusion(bf16[64,2,36,128]{3,1,2,0:T(2,128)(2,1)} %param.3), kind=kLoop, calls=%fused_computation.167 | loop fusion | bytes 2359296 | tf_op jit(solution)/shard_map/slice | solution.py:201
  5.3 1.9 %fusion.39 = (bf16[64,1,36,128]{3,2,1,0:T(8,128)(2,1)S(1)}, bf16[64,1,36,128]{3,2,1,0:T(8,128)(2,1)S(1)}, bf16[64,1,36,128]{3,2,1,0:T(8,128)(2,1)S(1)}, bf16[64,...) fusion(bf16[64,1,36,128]{3,2,1,0:T(8,128)(2,1)S(1)} %get-tuple-, ...), kind=kLoop, calls=%fused_computation.60 | loop fusion | flops 11206656 | bytes 6672384 | tf_op jit(solution)/shard_map/convert.6
  7.5 1.6 %fusion.9 = bf16[36,5,64,2,128]{4,0,2,3,1:T(8,128)(2,1)} fusion(bf16[64,1,36,128]{3,2,1,0:T(8,128)(2,1)S(1)} %get-tuple-element.27, bf16[64,1,36,128]{3,2,1,0:T(8,128)(2,1)S(1)} %get-tuple-element.28, bf16[1,36,2,36]{1,3,0,2:T(8,128)(2,1)S(1)} %maximum_bitcast_fusion.15, bf16[1,36,2,36]{1,3,0,2:T(8,128)(2,1)S(1)} %fusion.76), kind=kOutput, calls=%fused_computation.33 | convolution fusion | flops 87904512 | bytes 2500736 | tf_op jit(solution)/shard_map/npar,paqm->mnqr/dot_general | solution.py:207
  9.1 1.7 %fusion.11 = bf16[36,5,64,2,128]{4,0,2,3,1:T(8,128)(2,1)} fusion(bf16[36,5,64,2,128]{4,0,2,3,1:T(8,128)(2,1)} %fusion.9, bf16[64,1,36,128]{3,2,1,0:T(8,128)(2,1)S(1)} %get-tuple-element.23, bf16[64,1,36,128]{3,2,1,0:T(8,128)(2,1)S(1)} %get-tuple-element.24, bf16[1,36,2,36]{1,3,0,2:T(8,128)(2,1)S(1)} %maximum_bitcast_fusion.15, ...), kind=kOutput, calls=%fused_computation.35 | convolution fusion | flops 87904512 | bytes 2500736 | tf_op jit(solution)/shard_map/npar,paqm->mnqr/dot_general | solution.py:207
  10.7 1.6 %fusion.13 = bf16[36,5,64,2,128]{4,0,2,3,1:T(8,128)(2,1)} fusion(bf16[36,5,64,2,128]{4,0,2,3,1:T(8,128)(2,1)} %fusion.11, bf16[64,1,36,128]{3,2,1,0:T(8,128)(2,1)S(1)} %get-tuple-element.25, bf16[64,1,36,128]{3,2,1,0:T(8,128)(2,1)S(1)} %get-tuple-element.26, bf16[1,36,2,36]{1,3,0,2:T(8,128)(2,1)S(1)} %maximum_bitcast_fusion.15, ...), kind=kOutput, calls=%fused_computation.37 | convolution fusion | flops 87904512 | bytes 2500736 | tf_op jit(solution)/shard_map/npar,paqm->mnqr/dot_general | solution.py:207
  12.4 1.6 %fusion.15 = bf16[36,5,64,2,128]{4,0,2,3,1:T(8,128)(2,1)} fusion(bf16[36,5,64,2,128]{4,0,2,3,1:T(8,128)(2,1)} %fusion.13, bf16[64,1,36,128]{3,2,1,0:T(8,128)(2,1)S(1)} %get-tuple-element.14, bf16[64,1,36,128]{3,2,1,0:T(8,128)(2,1)S(1)} %get-tuple-element.13, bf16[1,36,2,36]{1,3,0,2:T(8,128)(2,1)S(1)} %maximum_bitcast_fusion.15, ...), kind=kOutput, calls=%fused_computation.39 | convolution fusion | flops 87904512 | bytes 2500736 | tf_op jit(solution)/shard_map/npar,paqm->mnqr/dot_general | solution.py:207
  14.0 1.7 %fusion.17 = bf16[36,5,64,2,128]{4,0,2,3,1:T(8,128)(2,1)} fusion(bf16[36,5,64,2,128]{4,0,2,3,1:T(8,128)(2,1)} %fusion.15, bf16[64,1,36,128]{3,2,1,0:T(8,128)(2,1)S(1)} %get-tuple-element.22, bf16[64,1,36,128]{3,2,1,0:T(8,128)(2,1)S(1)} %get-tuple-element.10, bf16[1,36,2,36]{1,3,0,2:T(8,128)(2,1)S(1)} %maximum_bitcast_fusion.15, ...), kind=kOutput, calls=%fused_computation.41 | convolution fusion | flops 87904512 | bytes 2500736 | tf_op jit(solution)/shard_map/npar,paqm->mnqr/dot_general | solution.py:207
  15.8 0.7 reshape.536
  16.5 11.7 %shard_map.50 = bf16[8,16,864]{2,1,0:T(8,128)(2,1)} custom-call(bf16[16,864]{1,0:T(8,128)(2,1)} %bitcast.184), custom_call_target="tpu_custom_call" | custom-call | tf_op jit(solution)/shard_map/pallas_call | solution.py:81
  28.3 1.7 %reshape.537 = bf16[128,12,2,36]{3,2,1,0:T(2,128)(2,1)S(1)} reshape(bf16[8,16,864]{2,1,0:T(8,128)(2,1)} %shard_map.50) | data formatting | bytes 442368 | tf_op jit(solution)/shard_map/reshape | solution.py:189
  30.0 0.9 %copy.37 = bf16[128,12,2,36]{0,3,2,1:T(8,128)(2,1)S(1)} copy(bf16[128,12,2,36]{3,2,1,0:T(2,128)(2,1)S(1)} %reshape.537) | data formatting | bytes 442368 | tf_op jit(solution)/shard_map/reshape | solution.py:189
  31.3 5.1 %fusion.4 = f32[5,64,36,24]{1,3,0,2:T(8,128)S(1)} fusion(bf16[36,5,64,2,128]{4,0,2,3,1:T(8,128)(2,1)} %fusion.17, bf16[36,2,128,24,1]{2,0,3,1,4:T(8,128)(2,1)S(1)} %maximum_bitcast_fusion.10), kind=kOutput, calls=%fused_computation.29 | convolution fusion | flops 141557760 | bytes 7446528 | tf_op jit(solution)/shard_map/msnqr,mqrd->snmd/dot_general | solution.py:212
  37.8 2.4 %fusion.25 = f32[64,5,12,36]{0,3,2,1:T(8,128)} fusion(f32[5,64,36,2,12]{1,2,4,3,0:T(8,128)S(1)} %bitcast.183, f32[12]{0:T(128)S(1)} %broadcast_multiply_fusion, f32[36,1,36]{0,2,1:T(8,128)S(1)} %get-tuple-element.58, f32[36,1,36]{0,2,1:T(8,128)S(1)} %get-tuple-element.57), kind=kOutput, calls=%fused_computation.46 | convolution fusion | flops 119582784 | bytes 1669296 | tf_op jit(solution)/shard_map/snmpc,mpk->nsck/dot_general | solution.py:215
  40.2 1.4 %reshape.539 = f32[64,2160]{0,1:T(8,128)S(1)} reshape(f32[64,5,12,36]{0,3,2,1:T(8,128)} %fusion.25) | data formatting | bytes 1105920 | tf_op jit(solution)/shard_map/reshape | solution.py:217
  41.5 1.2 %copy.44.x_ref = f32[64,2160]{1,0:T(8,128)} copy(f32[64,2160]{0,1:T(8,128)S(1)} %reshape.539) | data formatting | bytes 1105920 | tf_op jit(solution)/shard_map/reshape | solution.py:217
  42.7 6.6 %shard_map.51 = (f32[64,2160]{1,0:T(8,128)}, f32[64,128]{1,0:T(8,128)}) custom-call(f32[64,2160]{1,0:T(8,128)} %copy.44.x_ref), custom_call_target="tpu_custom_call" | custom-call | tf_op jit(solution)/shard_map/pallas_call | solution.py:160
  49.3 1.4 %copy.45 = f32[64,2160]{0,1:T(8,128)S(1)} copy(f32[64,2160]{1,0:T(8,128)} %get-tuple-element.6) | data formatting | bytes 1105920 | tf_op jit(solution)/shard_map/pallas_call | solution.py:160
  50.9 2.1 %fusion.18 = bf16[36,2,12,5,64,1]{4,0,2,3,1,5:T(8,128)(2,1)S(1)} fusion(f32[64,5,12,36,1]{0,3,2,1,4:T(8,128)S(1)} %reshape.561, f32[1,36,36]{2,1,0:T(8,128)S(1)} %get-tuple-element.59, f32[1,36,36]{2,1,0:T(8,128)S(1)} %get-tuple-element.60), kind=kOutput, calls=%fused_computation.42 | convolution fusion | flops 119718432 | bytes 1116288 | tf_op jit(solution)/shard_map/nsck,pmk->mpcsn/dot_general | solution.py:221
  52.9 4.0 %fusion.19 = f32[36,2,12,2,128]{4,2,3,1,0:T(8,128)S(1)} fusion(bf16[36,5,64,2,128,1]{4,0,2,3,1,5:T(8,128)(2,1)} %bitcast.50, bf16[36,2,12,5,64,1]{4,0,2,3,1,5:T(8,128)(2,1)S(1)} %fusion.18), kind=kOutput, calls=%fused_computation.44 | convolution fusion | flops 141557760 | bytes 7335936 | tf_op jit(solution)/shard_map/mpcsn,msnqr->mpcqr/dot_general | solution.py:224
  57.1 1.1 %copy.50 = bf16[128,12,2,36]{3,2,1,0:T(2,128)(2,1)S(1)} copy(bf16[128,12,2,36]{0,1,3,2:T(8,128)(2,1)S(1)} %maximum_bitcast_fusion.11) | data formatting | bytes 442368 | tf_op jit(solution)/shard_map/transpose | solution.py:228
  58.3 1.1 %reshape.541.x_ref = bf16[8,16,864]{2,1,0:T(8,128)(2,1)} reshape(bf16[128,12,2,36]{3,2,1,0:T(2,128)(2,1)S(1)} %copy.50) | data formatting | bytes 442368 | tf_op jit(solution)/shard_map/reshape | solution.py:228
  60.3 13.6 %shard_map.52 = (f32[16,864]{1,0:T(8,128)}, f32[8,12]{1,0:T(8,128)}) custom-call(bf16[8,16,864]{2,1,0:T(8,128)(2,1)} %reshape.541.x_ref, f32[8,12]{1,0:T(8,128)} %broadcast_in_dim.2.t_ref), custom_call_target="tpu_custom_call" | custom-call | tf_op jit(solution)/shard_map/pallas_call | solution.py:115
  73.9 1.1 %reshape.542 = f32[12,2,36,16]{2,1,0,3:T(2,128)S(1)} reshape(f32[864,16]{0,1:T(8,128)} %bitcast.185) | data formatting | bytes 110592 | tf_op jit(solution)/shard_map/reshape | solution.py:233
  75.9 0.8 %copy_multiply_fusion = f32[12,2,36,16]{2,3,1,0:T(8,128)} fusion(f32[12,2,36,16]{2,1,0,3:T(2,128)S(1)} %reshape.542, f32[12,16]{1,0:T(8,128)S(1)} %add_divide_fusion), kind=kLoop, calls=%fused_computation.98 | loop fusion | flops 13824 | bytes 111360 | tf_op jit(solution)/shard_map/mul | solution.py:237
  (43 shorter events, 5.6 us)
Async XLA Ops:
  14.0 1.7 %copy-start.2 = (bf16[12,2,36,16]{2,3,1,0:T(8,128)(2,1)S(1)}, bf16[12,2,36,16]{2,3,1,0:T(8,128)(2,1)}, u32[]{:S(2)}) copy-start(bf16[12,2,36,16]{2,3,1,0:T(8,128)(2,1)} %param.4) | copy-start | bytes 82948
  15.7 15.2 %copy-start.4 = (f32[128]{0:T(128)S(1)}, f32[128]{0:T(128)}, u32[]{:S(2)}) copy-start(f32[128]{0:T(128)} %param.5) | copy-start | bytes 1540
  36.4 0.9 %copy-start.1 = (bf16[8,16,864]{2,1,0:T(8,128)(2,1)S(1)}, bf16[8,16,864]{2,1,0:T(8,128)(2,1)}, u32[]{:S(2)}) copy-start(bf16[8,16,864]{2,1,0:T(8,128)(2,1)} %shard_map.50) | copy-start | bytes 663556
  57.1 2.3 %copy-start = (f32[64,2160]{1,0:T(8,128)S(1)}, f32[64,2160]{1,0:T(8,128)}, u32[]{:S(2)}) copy-start(f32[64,2160]{1,0:T(8,128)} %get-tuple-element.6) | copy-start | bytes 1658884
  58.3 18.4 %copy-start.3 = (f32[64,128]{1,0:T(8,128)S(1)}, f32[64,128]{1,0:T(8,128)}, u32[]{:S(2)}) copy-start(f32[64,128]{1,0:T(8,128)} %get-tuple-element.9) | copy-start | bytes 98308

commit v2 on v1

--- a/solution.py
+++ b/solution.py
@@ -2,6 +2,8 @@
 
 import jax
 import jax.numpy as jnp
+import ml_dtypes
+import numpy as np
 from jax import lax
 from jax.experimental import pallas as pl
 from jax.experimental.pallas import tpu as pltpu
@@ -13,14 +15,6 @@
 ridge_term = 0.5
 shift_x = (0.0, 1.0, -1.0, 0.0, 0.0)
 shift_y = (0.0, 0.0, 0.0, 1.0, -1.0)
-
-
-def phase_tables(angles, cycles, shift_index):
-    theta = 2.0 * jnp.pi * jnp.arange(angles, dtype=jnp.float32) / angles
-    radius = jnp.arange(cycles, dtype=jnp.float32) / (2.0 * cycles)
-    along = shift_x[shift_index] * jnp.cos(theta) + shift_y[shift_index] * jnp.sin(theta)
-    phase = -2.0 * jnp.pi * along[:, None] * radius[None, :]
-    return (jnp.cos(phase), jnp.sin(phase))
 
 
 def rotation_tables(angles):
@@ -68,28 +62,130 @@
     return copies
 
 
-def gather_kernel(axis, count, x_ref, o_ref, land, send_sem, recv_sem):
+def phase_constants(angles, cycles):
+    theta = (2.0 * np.pi * np.arange(angles) / angles).astype(np.float32)
+    radius = (np.arange(cycles) / (2.0 * cycles)).astype(np.float32)
+    straight, crossed = [], []
+    for dx, dy in zip(shift_x, shift_y):
+        along = dx * np.cos(theta) + dy * np.sin(theta)
+        phase = -2.0 * np.pi * along[:, None] * radius[None, :]
+        cosine, sine = np.cos(phase), np.sin(phase)
+        straight.append(np.concatenate([cosine, cosine], axis=1))
+        crossed.append(np.concatenate([-sine, sine], axis=1))
+    return np.stack(straight).astype(np.float32), np.stack(crossed).astype(np.float32)
+
+
+def odd_factor(count):
+    return count // 4
+
+
+def rounded_root(index, count):
+    turn = 2.0 * np.pi * (index % count) / count
+    cosine, sine = np.float32(np.cos(turn)), np.float32(np.sin(turn))
+    return float(cosine.astype(ml_dtypes.bfloat16)), float(sine.astype(ml_dtypes.bfloat16))
+
+
+def swapped(z):
+    half = z.shape[-1] // 2
+    return jnp.concatenate([z[..., half:], z[..., :half]], axis=-1)
+
+
+def turned(z):
+    half = z.shape[-1] // 2
+    return jnp.concatenate([z[..., half:], -z[..., :half]], axis=-1)
+
+
+def transform(load, middle, store, angles):
+    odd = odd_factor(angles)
+    inverse = pow(4, -1, odd)
+    quarter = pow(odd, -1, 4)
+    for second in range(odd):
+        z = [load((odd * first + 4 * second) % angles) for first in range(4)]
+        plus, minus = z[0] + z[2], z[0] - z[2]
+        other, differ = z[1] + z[3], turned(z[1] - z[3])
+        middle[0, second] = plus + other
+        middle[1, second] = minus + differ
+        middle[2, second] = plus - other
+        middle[3, second] = minus - differ
+    for first in range(4):
+        head = middle[first, 0]
+        pairs = odd // 2
+        even, uneven = [], []
+        for j in range(1, pairs + 1):
+            low, high = middle[first, j], middle[first, odd - j]
+            even.append(low + high)
+            uneven.append(turned(low - high))
+        total = head
+        for part in even:
+            total = total + part
+        store((odd * quarter * first) % angles, total)
+        for k in range(1, pairs + 1):
+            real, imag = head, None
+            for j in range(1, pairs + 1):
+                cosine, sine = rounded_root(k * j, odd)
+                real = real + cosine * even[j - 1]
+                term = sine * uneven[j - 1]
+                imag = term if imag is None else imag + term
+            base = odd * quarter * first
+            store((base + 4 * inverse * k) % angles, real + imag)
+            store((base + 4 * inverse * (odd - k)) % angles, real - imag)
+
+
+TILE = 16
+
+
+def spectra_kernel(
+    axis, count, w_ref, x_ref, c_ref, s_ref, o_ref, g_ref, land, middle, send_sem, recv_sem
+):
     me = greet(axis, count)
-    copies = push(axis, count, me, lambda peer: x_ref, land, send_sem, recv_sem)
-    land[me] = x_ref[...]
+    copies = push(axis, count, me, lambda peer: w_ref, land, send_sem, recv_sem)
+    land[me] = w_ref[...]
+    angles, particle_count = x_ref.shape[0], x_ref.shape[1]
+    tiles = particle_count // TILE
+
+    def step(index, carry):
+        shift = index // tiles
+        start = pl.multiple_of(lax.rem(index, tiles) * TILE, TILE)
+        target = pl.multiple_of(index * TILE, TILE)
+
+        def load(angle):
+            z = x_ref[angle, pl.ds(start, TILE), :].astype(jnp.float32)
+            straight = c_ref[shift, pl.ds(angle, 1), :]
+            crossed = s_ref[shift, pl.ds(angle, 1), :]
+            return z * straight + swapped(z) * crossed
+
+        def store(frequency, value):
+            o_ref[frequency, pl.ds(target, TILE), :] = value.astype(o_ref.dtype)
+
+        transform(load, middle, store, angles)
+        return carry
+
+    lax.fori_loop(0, SHIFTS * tiles, step, 0)
     for copy in copies:
         copy.wait()
-    o_ref[...] = land[...]
-
-
-def gather(axis, count, identity, x):
+    g_ref[...] = land[...]
+
+
+def spectra_and_gather(axis, count, identity, w, x, straight, crossed):
+    angles, particle_count, wide = x.shape
     return pl.pallas_call(
-        functools.partial(gather_kernel, axis, count),
-        out_shape=jax.ShapeDtypeStruct((count,) + x.shape, x.dtype),
-        in_specs=[pl.BlockSpec(memory_space=pltpu.VMEM)],
-        out_specs=pl.BlockSpec(memory_space=pltpu.VMEM),
+        functools.partial(spectra_kernel, axis, count),
+        out_shape=(
+            jax.ShapeDtypeStruct((angles, SHIFTS * particle_count, wide), jnp.bfloat16),
+            jax.ShapeDtypeStruct((count,) + w.shape, w.dtype),
+        ),
+        in_specs=[pl.BlockSpec(memory_space=pltpu.VMEM)] * 4,
+        out_specs=(pl.BlockSpec(memory_space=pltpu.VMEM),) * 2,
         scratch_shapes=[
-            pltpu.VMEM((count,) + x.shape, x.dtype),
+            pltpu.VMEM((count,) + w.shape, w.dtype),
+            pltpu.VMEM((4, odd_factor(angles), TILE, wide), jnp.float32),
             pltpu.SemaphoreType.DMA((count,)),
             pltpu.SemaphoreType.DMA((count,)),
         ],
-        compiler_params=pltpu.CompilerParams(collective_id=identity, has_side_effects=True),
-    )(x)
+        compiler_params=pltpu.CompilerParams(
+            collective_id=identity, has_side_effects=True, vmem_limit_bytes=40 * 1024 * 1024
+        ),
+    )(w, x, straight, crossed)
 
 
 def scatter_kernel(
@@ -186,7 +282,11 @@
 
     own = references.reshape(wide, cycle_count).T
     own = jnp.pad(own, ((0, rows - cycle_count), (0, 0)))
-    whole = gather("dom", dom, 0, own)[:, :cycle_count].reshape(cycles, classes, 2, angles)
+    arranged = jnp.transpose(particles, (2, 0, 1, 3)).reshape(angles, particle_count, 2 * cycles)
+    straight, crossed = phase_constants(angles, cycles)
+    spectra, whole = spectra_and_gather("dom", dom, 0, own, arranged, straight, crossed)
+    spectra = spectra.reshape(angles, SHIFTS, particle_count, 2, cycles)
+    whole = whole[:, :cycle_count].reshape(cycles, classes, 2, angles)
     whole_wide = whole.astype(jnp.float32)
     ref_spectra = jnp.einsum("rcpa,paqm->mqrc", whole, table, preferred_element_type=jnp.float32)
     weighted = (noise_weights[None, None, :, None] * ref_spectra).astype(jnp.bfloat16)
@@ -195,20 +295,6 @@
         [weighted, jnp.stack([-weighted[:, 1], weighted[:, 0]], axis=1)], axis=3
     )
 
-    spectra_list = []
-    for shift_index in range(SHIFTS):
-        cosine, sine = phase_tables(angles, cycles, shift_index)
-        real_part = particles[:, 0].astype(jnp.float32)
-        imag_part = particles[:, 1].astype(jnp.float32)
-        shifted = jnp.stack(
-            [real_part * cosine - imag_part * sine, real_part * sine + imag_part * cosine], axis=1
-        ).astype(jnp.bfloat16)
-        spectra_list.append(
-            jnp.einsum(
-                "npar,paqm->mnqr", shifted, table, preferred_element_type=jnp.float32
-            ).astype(jnp.bfloat16)
-        )
-    spectra = jnp.stack(spectra_list, axis=1)
     correlation = jnp.einsum("msnqr,mqrd->snmd", spectra, stacked, preferred_element_type=jnp.float32)
     turn = jnp.stack([cosine_k, -sine_k], axis=1) / angles
     both_parts = correlation.reshape(SHIFTS, particle_count, angles, 2, classes)

time: 77.9 us -> 80 us (1.027)
  local copies, waits for them, and re-layouts: 17.7 us -> 31.5 us
  matrix products: 22.1 us -> 13.4 us
  other arithmetic: 4.71 us -> 1.92 us
    reshape x2 -> x5, local copies, waits for them, and re-layouts: 2.58 us -> 16.8 us  [the longest x1 11.9 us: per_device(): spectra = spectra.reshape(angles, SHIFTS, particle_count, 2, cycles)]
    dot_general x5 -> x0, matrix products: 8.26 us -> none  [per_device(): jnp.einsum('npar,paqm->mnqr', shifted, table, preferred_element_type=jnp....]
    unnamed x11 -> x13, local copies, waits for them, and re-layouts: 0.53 us -> 4.29 us
    slice x1 -> x0, local copies, waits for them, and re-layouts: 3.74 us -> none  [per_device(): real_part = particles[:, 0].astype(jnp.float32)]
    another operation x3 -> x1, other arithmetic: 2.31 us -> 0.11 us
    pallas_call x1, Pallas kernels: 13.6 us -> 11.9 us  [scatter(): pl.pallas_call(functools.partial(scatter_kernel, axis, count), out_shape=...]
    pallas_call x1, Pallas kernels: 11.7 us -> 13 us  [spectra_and_gather(): pl.pallas_call(functools.partial(spectra_kernel, axis, count), out_shape=...]
where the time goes in v2:
time: 80 us; the launch traced here: 79.2 us
  local copies, waits for them, and re-layouts  31.5 us (39%)
  Pallas kernels  31.5 us (39%)
  matrix products  13.4 us (17%)
  other arithmetic  1.92 us (2%)
  between operations  0.88 us (1%)
    pallas_call x1, Pallas kernels, spectra_and_gather(): pl.pallas_call(functools.partial(spectra_kernel, axis, count), out_shape=...  13 us
    pallas_call x1, Pallas kernels, scatter(): pl.pallas_call(functools.partial(scatter_kernel, axis, count), out_shape=...  11.9 us
    reshape x1, local copies, waits for them, and re-layouts, per_device(): spectra = spectra.reshape(angles, SHIFTS, particle_count, 2, cycles)  11.9 us
    pallas_call x1, Pallas kernels, posteriors(): pl.pallas_call(functools.partial(posterior_kernel, axis, count), out_shap...  6.55 us
    dot_general x1, matrix products, per_device(): jnp.einsum('msnqr,mqrd->snmd', spectra, stacked, preferred_element_type=j...  4.93 us
    unnamed x13, local copies, waits for them, and re-layouts  4.29 us
    dot_general x1, matrix products, per_device(): jnp.einsum('mpcsn,msnqr->mpcqr', both, spectra, preferred_element_type=jn...  3.8 us
    reshape x2, local copies, waits for them, and re-layouts, per_device(): jnp.transpose(particles, (2, 0, 1, 3))  3.44 us

profile of v2, /device:TPU:0, one launch (start us, length us, event | category | flops | bytes accessed | tf_op | source)
XLA Modules:
  0.0 79.2 jit_solution(1718535601430105229)
XLA Ops:
  0.6 1.0 %copy.36 = bf16[12,2,36,16]{2,1,0,3:T(2,128)(2,1)S(1)} copy(bf16[12,2,36,16]{2,3,1,0:T(8,128)(2,1)} %param.6) | data formatting | bytes 55296 | tf_op args[1]
  1.7 3.2 %reshape.251 = bf16[36,64,256]{2,0,1:T(8,128)(2,1)S(1)} reshape(bf16[36,64,2,128]{3,2,0,1:T(2,128)(2,1)} %bitcast.104) | data formatting | bytes 2359296 | tf_op jit(solution)/shard_map/reshape | solution.py:285
  5.2 0.6 copy-done.1
  5.9 13.0 %shard_map.68 = (bf16[36,320,256]{2,1,0:T(8,128)(2,1)S(1)}, bf16[8,16,864]{2,1,0:T(8,128)(2,1)S(1)}) custom-call(bf16[16,864]{1,0:T(8,128)(2,1)S(1)} %bitcast.101, bf16[36,64,256]{2,1,0:T(8,128)(2,1)S(1)} %copy.61.x_ref, f32[5,36,256]{2,1,0:T(8,128)S(1)} %copy-done.1, f32[5,36,256]{2,1,0:T(8,128)S(1)} %copy-done.2), custom_call_target="tpu_custom_call" | custom-call | tf_op jit(solution)/shard_map/pallas_call | solution.py:171
  18.9 2.6 %copy-done = bf16[36,320,256]{2,1,0:T(8,128)(2,1)} copy-done((bf16[36,320,256]{2,1,0:T(8,128)(2,1)}, bf16[36,320,256]{2,1,0:T(8,128)(2,1)S(1)}, u32[]{:S(2)}) %copy-start) | copy-done | bytes 5898264
  21.5 11.9 %reshape.233 = bf16[36,5,64,2,128]{4,3,2,1,0:T(2,128)(2,1)} reshape(bf16[36,320,256]{2,1,0:T(8,128)(2,1)} %copy-done) | data formatting | bytes 11796480 | tf_op jit(solution)/shard_map/reshape | solution.py:288
  33.4 0.7 reshape.232
  34.1 0.7 copy.38
  35.5 4.9 %fusion.4 = f32[5,64,36,24]{1,3,0,2:T(8,128)S(1)} fusion(bf16[36,5,64,2,128]{4,3,2,1,0:T(2,128)(2,1)} %reshape.233, bf16[36,2,128,24,1]{2,0,3,1,4:T(8,128)(2,1)S(1)} %maximum_bitcast_fusion), kind=kOutput, calls=%fused_computation.4 | convolution fusion | flops 141557760 | bytes 7446528 | tf_op jit(solution)/shard_map/msnqr,mqrd->snmd/dot_general | solution.py:298
  41.4 2.4 %fusion.15 = f32[64,5,12,36]{0,3,2,1:T(8,128)} fusion(f32[5,64,36,2,12]{1,2,4,3,0:T(8,128)S(1)} %bitcast.103, f32[12]{0:T(128)S(1)} %broadcast_multiply_fusion, f32[36,1,36]{0,2,1:T(8,128)S(1)} %get-tuple-element.19, f32[36,1,36]{0,2,1:T(8,128)S(1)} %get-tuple-element.18), kind=kOutput, calls=%fused_computation.11 | convolution fusion | flops 119582784 | bytes 1669296 | tf_op jit(solution)/shard_map/snmpc,mpk->nsck/dot_general | solution.py:301
  43.8 1.6 %reshape.235 = f32[64,2160]{0,1:T(8,128)S(1)} reshape(f32[64,5,12,36]{0,3,2,1:T(8,128)} %fusion.15) | data formatting | bytes 1105920 | tf_op jit(solution)/shard_map/reshape | solution.py:303
  45.4 1.2 %copy.43.x_ref = f32[64,2160]{1,0:T(8,128)} copy(f32[64,2160]{0,1:T(8,128)S(1)} %reshape.235) | data formatting | bytes 1105920 | tf_op jit(solution)/shard_map/reshape | solution.py:303
  46.5 6.5 %shard_map.69 = (f32[64,2160]{1,0:T(8,128)}, f32[64,128]{1,0:T(8,128)}) custom-call(f32[64,2160]{1,0:T(8,128)} %copy.43.x_ref), custom_call_target="tpu_custom_call" | custom-call | tf_op jit(solution)/shard_map/pallas_call | solution.py:256
  53.1 1.4 %copy.44 = f32[64,2160]{0,1:T(8,128)S(1)} copy(f32[64,2160]{1,0:T(8,128)} %get-tuple-element.10) | data formatting | bytes 1105920 | tf_op jit(solution)/shard_map/pallas_call | solution.py:256
  54.7 2.1 %fusion.8 = bf16[36,2,12,5,64,1]{4,0,2,3,1,5:T(8,128)(2,1)S(1)} fusion(f32[64,5,12,36,1]{0,3,2,1,4:T(8,128)S(1)} %reshape.247, f32[1,36,36]{2,1,0:T(8,128)S(1)} %get-tuple-element.20, f32[1,36,36]{2,1,0:T(8,128)S(1)} %get-tuple-element.21), kind=kOutput, calls=%fused_computation.7 | convolution fusion | flops 119718432 | bytes 1116288 | tf_op jit(solution)/shard_map/nsck,pmk->mpcsn/dot_general | solution.py:307
  56.8 3.8 %fusion.9 = f32[36,2,12,2,128]{4,2,3,1,0:T(8,128)S(1)} fusion(bf16[36,5,64,2,128,1]{4,3,2,1,0,5:T(2,128)(2,1)} %bitcast.102, bf16[36,2,12,5,64,1]{4,0,2,3,1,5:T(8,128)(2,1)S(1)} %fusion.8), kind=kOutput, calls=%fused_computation.9 | convolution fusion | flops 141557760 | bytes 7335936 | tf_op jit(solution)/shard_map/mpcsn,msnqr->mpcqr/dot_general | solution.py:310
  60.8 1.1 %copy.49 = bf16[128,12,2,36]{3,2,1,0:T(2,128)(2,1)S(1)} copy(bf16[128,12,2,36]{0,1,3,2:T(8,128)(2,1)S(1)} %maximum_bitcast_fusion.1) | data formatting | bytes 442368 | tf_op jit(solution)/shard_map/transpose | solution.py:314
  61.9 1.1 %reshape.237.x_ref = bf16[8,16,864]{2,1,0:T(8,128)(2,1)} reshape(bf16[128,12,2,36]{3,2,1,0:T(2,128)(2,1)S(1)} %copy.49) | data formatting | bytes 442368 | tf_op jit(solution)/shard_map/reshape | solution.py:314
  63.3 0.6 broadcast_in_dim.2.t_ref
  63.9 11.9 %shard_map.70 = (f32[16,864]{1,0:T(8,128)}, f32[8,12]{1,0:T(8,128)}) custom-call(bf16[8,16,864]{2,1,0:T(8,128)(2,1)} %reshape.237.x_ref, f32[8,12]{1,0:T(8,128)} %broadcast_in_dim.2.t_ref), custom_call_target="tpu_custom_call" | custom-call | tf_op jit(solution)/shard_map/pallas_call | solution.py:211
  75.8 1.1 %reshape.238 = f32[12,2,36,16]{2,1,0,3:T(2,128)S(1)} reshape(f32[864,16]{0,1:T(8,128)} %bitcast.105) | data formatting | bytes 110592 | tf_op jit(solution)/shard_map/reshape | solution.py:319
  77.0 0.7 slice_bitcast_fusion.2
  77.8 0.8 copy_multiply_fusion
  78.6 0.6 slice_reduce_fusion
  (35 shorter events, 2.8 us)
Async XLA Ops:
  4.9 0.9 %copy-start.1 = (f32[5,36,256]{2,1,0:T(8,128)S(1)}, f32[5,36,256]{2,1,0:T(8,128)}, u32[]{:S(2)}) copy-start(f32[5,36,256]{2,1,0:T(8,128)} %constant.43.clone.c_ref) | copy-start | bytes 552964
  4.9 1.0 %copy-start.2 = (f32[5,36,256]{2,1,0:T(8,128)S(1)}, f32[5,36,256]{2,1,0:T(8,128)}, u32[]{:S(2)}) copy-start(f32[5,36,256]{2,1,0:T(8,128)} %constant.44.clone.s_ref) | copy-start | bytes 552964
  18.9 2.6 %copy-start = (bf16[36,320,256]{2,1,0:T(8,128)(2,1)}, bf16[36,320,256]{2,1,0:T(8,128)(2,1)S(1)}, u32[]{:S(2)}) copy-start(bf16[36,320,256]{2,1,0:T(8,128)(2,1)S(1)} %get-tuple-element.9) | copy-start | bytes 17694724
  33.4 1.7 %copy-start.5 = (f32[128]{0:T(128)S(1)}, f32[128]{0:T(128)}, u32[]{:S(2)}) copy-start(f32[128]{0:T(128)} %param.7) | copy-start | bytes 1540
  60.7 2.3 %copy-start.3 = (f32[64,2160]{1,0:T(8,128)S(1)}, f32[64,2160]{1,0:T(8,128)}, u32[]{:S(2)}) copy-start(f32[64,2160]{1,0:T(8,128)} %get-tuple-element.10) | copy-start | bytes 1658884
  61.9 16.7 %copy-start.4 = (f32[64,128]{1,0:T(8,128)S(1)}, f32[64,128]{1,0:T(8,128)}, u32[]{:S(2)}) copy-start(f32[64,128]{1,0:T(8,128)} %get-tuple-element.13) | copy-start | bytes 98308

commit v3 on v2

v3 whole, which is shorter than its diff:
```python
import functools

import jax
import jax.numpy as jnp
import ml_dtypes
import numpy as np
from jax import lax
from jax.experimental import pallas as pl
from jax.experimental.pallas import tpu as pltpu
from jax.sharding import PartitionSpec as P

SHIFTS = 5
MESH = pl.DeviceIdType.MESH

ridge_term = 0.5
shift_x = (0.0, 1.0, -1.0, 0.0, 0.0)
shift_y = (0.0, 0.0, 0.0, 1.0, -1.0)


def rotation_tables(angles):
    steps = jnp.arange(angles, dtype=jnp.int32)
    product = steps[:, None] * steps[None, :] % angles
    turn = 2.0 * jnp.pi * product.astype(jnp.float32) / angles
    return (jnp.cos(turn), jnp.sin(turn))


def angular_table(angles):
    cosine, sine = rotation_tables(angles)
    upper = jnp.stack([cosine, -sine], axis=1)
    lower = jnp.stack([sine, cosine], axis=1)
    return jnp.stack([upper, lower], axis=0).astype(jnp.bfloat16)


def greet(counts):
    barrier = pltpu.get_barrier_semaphore()
    for axis, count in counts.items():
        me = lax.axis_index(axis)
        for step in range(1, count):
            pl.semaphore_signal(
                barrier,
                inc=1,
                device_id={axis: lax.rem(me + step, count)},
                device_id_type=MESH,
            )
    pl.semaphore_wait(barrier, sum(counts.values()) - len(counts))


def push(axis, count, me, source, land, send_sem, recv_sem):
    copies = []
    for step in range(1, count):
        peer = lax.rem(me + step, count)
        copy = pltpu.make_async_remote_copy(
            src_ref=source(peer),
            dst_ref=land.at[me],
            send_sem=send_sem.at[step],
            recv_sem=recv_sem.at[step],
            device_id={axis: peer},
            device_id_type=MESH,
        )
        copy.start()
        copies.append(copy)
    return copies


def phase_constants(angles, cycles):
    theta = (2.0 * np.pi * np.arange(angles) / angles).astype(np.float32)
    radius = (np.arange(cycles) / (2.0 * cycles)).astype(np.float32)
    straight, crossed = [], []
    for dx, dy in zip(shift_x, shift_y):
        along = dx * np.cos(theta) + dy * np.sin(theta)
        phase = -2.0 * np.pi * along[:, None] * radius[None, :]
        cosine, sine = np.cos(phase), np.sin(phase)
        straight.append(np.concatenate([cosine, cosine], axis=1))
        crossed.append(np.concatenate([-sine, sine], axis=1))
    return np.stack(straight).astype(np.float32), np.stack(crossed).astype(np.float32)


def odd_factor(count):
    return count // 4


def full_root(index, count):
    turn = 2.0 * np.pi * (index % count) / count
    return float(np.cos(turn)), float(np.sin(turn))


def rounded_root(index, count):
    turn = 2.0 * np.pi * (index % count) / count
    cosine, sine = np.float32(np.cos(turn)), np.float32(np.sin(turn))
    return float(cosine.astype(ml_dtypes.bfloat16)), float(sine.astype(ml_dtypes.bfloat16))


def swapped(z):
    half = z.shape[-1] // 2
    return jnp.concatenate([z[..., half:], z[..., :half]], axis=-1)


def turned(z, axis):
    low, high = jnp.split(z, 2, axis=axis)
    return jnp.concatenate([high, -low], axis=axis)


def transform(load, middle, store, angles, root, axis):
    odd = odd_factor(angles)
    inverse = pow(4, -1, odd)
    quarter = pow(odd, -1, 4)
    for second in range(odd):
        z = [load((odd * first + 4 * second) % angles) for first in range(4)]
        plus, minus = z[0] + z[2], z[0] - z[2]
        other, differ = z[1] + z[3], turned(z[1] - z[3], axis)
        middle[0, second] = plus + other
        middle[1, second] = minus + differ
        middle[2, second] = plus - other
        middle[3, second] = minus - differ
    for first in range(4):
        head = middle[first, 0]
        pairs = odd // 2
        even, uneven = [], []
        for j in range(1, pairs + 1):
            low, high = middle[first, j], middle[first, odd - j]
            even.append(low + high)
            uneven.append(turned(low - high, axis))
        total = head
        for part in even:
            total = total + part
        store((odd * quarter * first) % angles, total)
        for k in range(1, pairs + 1):
            real, imag = head, None
            for j in range(1, pairs + 1):
                cosine, sine = root(k * j, odd)
                real = real + cosine * even[j - 1]
                term = sine * uneven[j - 1]
                imag = term if imag is None else imag + term
            base = odd * quarter * first
            store((base + 4 * inverse * k) % angles, real + imag)
            store((base + 4 * inverse * (odd - k)) % angles, real - imag)


TILE = 16
BLOCK = 128


def em_kernel(
    dom, cls, classes,
    w_ref, h_ref, x_ref, c_ref, s_ref,
    o_ref, u_ref, e_ref,
    spectra, w_land, h_land, turned_w, middle, corr, wide_middle, scores, weights,
    stat, stat_land, sums, outgoing, land, total_block, total_land,
    w_send, w_recv, h_send, h_recv, stat_send, stat_recv, o_send, o_recv, t_send, t_recv,
):
    greet({"dom": dom, "cls": cls})
    me, column = lax.axis_index("dom"), lax.axis_index("cls")
    copies = push("dom", dom, me, lambda peer: w_ref, w_land, w_send, w_recv)
    copies += push("dom", dom, me, lambda peer: h_ref, h_land, h_send, h_recv)
    w_land[me] = w_ref[...]
    h_land[me] = h_ref[...]
    angles, particle_count, width = x_ref.shape
    cycles = width // 2
    cycle_count = cycles // dom
    tiles = particle_count // TILE
    padded = scores.shape[1]
    pairs = 2 * classes

    def step(index, carry):
        shift = index // tiles
        start = pl.multiple_of(lax.rem(index, tiles) * TILE, TILE)
        target = pl.multiple_of(index * TILE, TILE)

        def load(angle):
            z = x_ref[angle, pl.ds(start, TILE), :].astype(jnp.float32)
            straight = c_ref[shift, pl.ds(angle, 1), :]
            crossed = s_ref[shift, pl.ds(angle, 1), :]
            return z * straight + swapped(z) * crossed

        def store(frequency, value):
            spectra[frequency, pl.ds(target, TILE), :] = value.astype(spectra.dtype)

        transform(load, middle, store, angles, rounded_root, 1)
        return carry

    lax.fori_loop(0, SHIFTS * tiles, step, 0)

    for copy in copies:
        copy.wait()
    half_norms = h_land[0]
    for index in range(1, dom):
        half_norms = half_norms + h_land[index]
    row = lax.broadcasted_iota(jnp.int32, half_norms.shape, 0)
    half_norms = jnp.where(row < classes, 0.5 * half_norms, 1e30)[:, 0:1]
    for block in range(turned_w.shape[0] // BLOCK):
        lanes = slice(block * BLOCK, (block + 1) * BLOCK)
        piece = jnp.concatenate(
            [w_land[index][:, lanes].astype(jnp.float32)[:cycle_count] for index in range(dom)], axis=0
        )
        turned_w[lanes, :] = piece.T

    def correlate(m, carry):
        both = turned_w[pl.ds(pl.multiple_of(m * pairs, 8), pairs), :]
        gap = jnp.zeros((padded - classes, cycles), jnp.float32)
        real = jnp.concatenate([both[:classes], gap], axis=0)
        imag = jnp.concatenate([both[classes:], gap], axis=0)
        left = jnp.concatenate([real, imag], axis=0)
        right = jnp.concatenate([imag, -real], axis=0)
        stacked = jnp.concatenate([left, right], axis=1).astype(jnp.bfloat16)
        corr[m] = lax.dot_general(
            stacked, spectra[m], (((1,), (1,)), ((), ())), preferred_element_type=jnp.float32
        )
        return carry

    lax.fori_loop(0, angles, correlate, 0)

    def keep_score(k, value):
        scores[k] = value[:padded] * (1.0 / angles) - half_norms

    transform(lambda m: corr[m], wide_middle, keep_score, angles, full_root, 0)

    def fold(values, combine):
        parts = [
            values[:, index * particle_count : (index + 1) * particle_count] for index in range(SHIFTS)
        ]
        return functools.reduce(combine, parts)

    def spread(values):
        return jnp.concatenate([values] * SHIFTS, axis=1)

    highest = lax.fori_loop(1, angles, lambda k, best: jnp.maximum(best, scores[k]), scores[0])
    peak = fold(jnp.max(highest, axis=0, keepdims=True), jnp.maximum)
    wide_peak = spread(peak)

    def exponentiate(k, total):
        value = jnp.exp(scores[k] - wide_peak)
        scores[k] = value
        return total + value

    class_total = lax.fori_loop(0, angles, exponentiate, jnp.zeros(scores.shape[1:], jnp.float32))
    total = fold(jnp.sum(class_total, axis=0, keepdims=True), jnp.add)
    row = lax.broadcasted_iota(jnp.int32, stat.shape, 0)
    stat[...] = jnp.where(row == 0, peak, total)
    copies = push("cls", cls, column, lambda peer: stat, stat_land, stat_send, stat_recv)
    stat_land[column] = stat[...]
    for copy in copies:
        copy.wait()
    peaks = stat_land[0][0:1]
    for index in range(1, cls):
        peaks = jnp.maximum(peaks, stat_land[index][0:1])
    totals = jnp.zeros_like(peaks)
    for index in range(cls):
        part = stat_land[index]
        totals = totals + part[1:2] * jnp.exp(part[0:1] - peaks)
    scale = spread(jnp.exp(peak - peaks) / totals)
    e_ref[...] = jnp.broadcast_to(peaks + jnp.log(totals), e_ref.shape)
    weight = jnp.sum(class_total * scale, axis=1, keepdims=True)
    total_block[...] = jnp.broadcast_to(weight, total_block.shape)
    copies = push("dom", dom, me, lambda peer: total_block, total_land, t_send, t_recv)
    total_land[me] = total_block[...]

    def load_posterior(k):
        value = scores[k] * scale
        return jnp.concatenate([value, jnp.zeros_like(value)], axis=0)

    def keep_weight(m, value):
        weights[m] = jnp.concatenate([value[:padded], -value[padded:]], axis=0).astype(weights.dtype)

    transform(load_posterior, wide_middle, keep_weight, angles, full_root, 0)

    used = angles * pairs
    if sums.shape[0] > used:
        sums[used:] = jnp.zeros((sums.shape[0] - used, cycles), jnp.float32)

    def accumulate(m, carry):
        parts = jnp.dot(weights[m], spectra[m], preferred_element_type=jnp.float32)
        real = parts[:padded, :cycles] - parts[padded:, cycles:]
        imag = parts[:padded, cycles:] + parts[padded:, :cycles]
        sums[pl.ds(pl.multiple_of(m * pairs, 8), pairs), :] = jnp.concatenate(
            [real[:classes], imag[:classes]], axis=0
        )
        return carry

    lax.fori_loop(0, angles, accumulate, 0)
    rows = outgoing.shape[1]
    for block in range(sums.shape[0] // BLOCK):
        lanes = slice(block * BLOCK, (block + 1) * BLOCK)
        piece = sums[lanes, :].T
        for index in range(dom):
            part = piece[index * cycle_count : (index + 1) * cycle_count]
            if rows > cycle_count:
                gap = jnp.zeros((rows - cycle_count, BLOCK), jnp.float32)
                part = jnp.concatenate([part, gap], axis=0)
            outgoing[index, :, lanes] = part.astype(outgoing.dtype)
    copies += push("dom", dom, me, lambda peer: outgoing.at[peer], land, o_send, o_recv)
    land[me] = outgoing[me]
    for copy in copies:
        copy.wait()
    result = land[0].astype(jnp.float32)
    weight = total_land[0]
    for index in range(1, dom):
        result = result + land[index].astype(jnp.float32)
        weight = weight + total_land[index]
    o_ref[...] = result
    u_ref[...] = weight


def em_step(dom, cls, classes, w, h, x, straight, crossed):
    angles, particle_count, width = x.shape
    cycles = width // 2
    rows, long = w.shape
    padded = h.shape[0]
    images = SHIFTS * particle_count
    odd = odd_factor(angles)
    f32, b16 = jnp.float32, jnp.bfloat16
    scratch = [
        pltpu.VMEM((angles, images, width), b16),
        pltpu.VMEM((dom, rows, long), b16),
        pltpu.VMEM((dom,) + h.shape, f32),
        pltpu.VMEM((long, cycles), f32),
        pltpu.VMEM((4, odd, TILE, width), f32),
        pltpu.VMEM((angles, 2 * padded, images), f32),
        pltpu.VMEM((4, odd, 2 * padded, images), f32),
        pltpu.VMEM((angles, padded, images), f32),
        pltpu.VMEM((angles, 2 * padded, images), b16),
        pltpu.VMEM((8, particle_count), f32),
        pltpu.VMEM((cls, 8, particle_count), f32),
        pltpu.VMEM((long, cycles), f32),
        pltpu.VMEM((dom, rows, long), b16),
        pltpu.VMEM((dom, rows, long), b16),
        pltpu.VMEM((padded, BLOCK), f32),
        pltpu.VMEM((dom, padded, BLOCK), f32),
    ]
    for count in (dom, dom, cls, dom, dom):
        scratch += [pltpu.SemaphoreType.DMA((count,))] * 2
    return pl.pallas_call(
        functools.partial(em_kernel, dom, cls, classes),
        out_shape=(
            jax.ShapeDtypeStruct((rows, long), f32),
            jax.ShapeDtypeStruct((padded, BLOCK), f32),
            jax.ShapeDtypeStruct((8, particle_count), f32),
        ),
        in_specs=[pl.BlockSpec(memory_space=pltpu.VMEM)] * 5,
        out_specs=(pl.BlockSpec(memory_space=pltpu.VMEM),) * 3,
        scratch_shapes=scratch,
        compiler_params=pltpu.CompilerParams(
            collective_id=0, has_side_effects=True, vmem_limit_bytes=40 * 1024 * 1024
        ),
    )(w, h, x, straight, crossed)


def per_device(dom, cls, particles, references, noise_weights):
    particle_count, _, angles, cycles = particles.shape
    classes = references.shape[0]
    cycle_count = cycles // dom
    rows = -(-cycle_count // 16) * 16
    padded = -(-classes // 8) * 8
    used = classes * 2 * angles
    long = -(-used // BLOCK) * BLOCK
    table = angular_table(angles)
    cycle_start = lax.axis_index("dom") * cycle_count
    noise = lax.dynamic_slice_in_dim(noise_weights, cycle_start, cycle_count, 0)

    ref_spectra = jnp.einsum(
        "cpar,paqm->rmqc", references, table, preferred_element_type=jnp.float32
    )
    weighted = (noise[:, None, None, None] * ref_spectra).astype(jnp.bfloat16)
    weighted = jnp.pad(
        weighted.reshape(cycle_count, used), ((0, rows - cycle_count), (0, long - used))
    )
    own_wide = references.astype(jnp.float32)
    norms = jnp.sum(noise * own_wide * own_wide, axis=(1, 2, 3))
    norms = jnp.broadcast_to(jnp.pad(norms, (0, padded - classes))[:, None], (padded, BLOCK))
    arranged = jnp.transpose(particles, (2, 0, 1, 3)).reshape(angles, particle_count, 2 * cycles)
    straight, crossed = phase_constants(angles, cycles)
    own_sums, own_weights, evidence = em_step(
        dom, cls, classes, weighted, norms, arranged, straight, crossed
    )
    own_sums = own_sums[:cycle_count, :used].reshape(cycle_count, angles, 2, classes)
    own_sums = jnp.transpose(own_sums, (3, 2, 1, 0))
    denominator = noise * own_weights[:classes, 0:1] + ridge_term
    class_spectra = own_sums * (noise / denominator)[:, None, None, :]
    return (class_spectra, evidence[0])


def solution(mesh):
    dom, cls = mesh.shape["dom"], mesh.shape["cls"]
    return jax.shard_map(
        functools.partial(per_device, dom, cls),
        mesh=mesh,
        in_specs=(P("dom", None, None, None), P("cls", None, None, "dom"), P()),
        out_specs=(P("cls", None, None, "dom"), P("dom")),
        check_vma=False,
    )
```

time: 80 us -> 47.1 us (0.59)
  local copies, waits for them, and re-layouts: 31.5 us -> 5.72 us
  matrix products: 13.4 us -> 1.11 us
  Pallas kernels: 31.5 us -> 37.7 us
    reshape x9 -> x2, local copies, waits for them, and re-layouts: 18.5 us -> 1 us  [the longest x1 0.8 us: per_device(): own_sums[:cycle_count, :used].reshape(cycle_count, angles, 2, classes)]
    dot_general x5 -> x1, matrix products: 13.4 us -> 1.11 us  [per_device(): jnp.einsum('cpar,paqm->rmqc', references, table, preferred_element_type=j...]
    pallas_call x3 -> x1, Pallas kernels: 31.5 us -> 37.7 us  [em_step(): pl.pallas_call(functools.partial(em_kernel, dom, cls, classes), out_shape...]
    unnamed x13 -> x7, local copies, waits for them, and re-layouts: 4.29 us -> 1.77 us
    reshape x2, local copies, waits for them, and re-layouts: 3.44 us -> 1.07 us  [per_device(): jnp.transpose(particles, (2, 0, 1, 3))]
    transpose x2 -> x0, local copies, waits for them, and re-layouts: 1.54 us -> none  [the longest x1 1.12 us: per_device(): sums = jnp.transpose(sums, (3, 1, 2, 0)).reshape(dom, cycle_count, wide)]
    pallas_call x1 -> x0, local copies, waits for them, and re-layouts: 1.42 us -> none  [posteriors(): pl.pallas_call(functools.partial(posterior_kernel, axis, count), out_shap...]
where the time goes in v3:
time: 47.1 us; the launch traced here: 46.9 us
  Pallas kernels  37.7 us (80%)
  local copies, waits for them, and re-layouts  5.72 us (12%)
  other arithmetic  1.65 us (4%)
  matrix products  1.11 us (2%)
  between operations  0.74 us (2%)
    pallas_call x1, Pallas kernels, em_step(): pl.pallas_call(functools.partial(em_kernel, dom, cls, classes), out_shape...  37.7 us
    unnamed x7, local copies, waits for them, and re-layouts  1.77 us
    reduce_sum x1, other arithmetic, per_device(): norms = jnp.sum(noise * own_wide * own_wide, axis=(1, 2, 3))  1.12 us
    dot_general x1, matrix products, per_device(): jnp.einsum('cpar,paqm->rmqc', references, table, preferred_element_type=j...  1.11 us
    reshape x2, local copies, waits for them, and re-layouts, per_device(): jnp.transpose(particles, (2, 0, 1, 3))  1.07 us

profile of v3, /device:TPU:0, one launch (start us, length us, event | category | flops | bytes accessed | tf_op | source)
XLA Modules:
  0.0 46.9 jit_solution(4264648762883115207)
XLA Ops:
  0.6 0.0 copy-start.2
  0.6 0.8 %dynamic_slice.3 = f32[16]{0:T(128)S(1)} dynamic-slice(f32[128]{0:T(128)} %param.7, s32[]{:T(128)S(6)} %select_n.31), dynamic_slice_sizes={16} | dynamic-slice | bytes 132 | tf_op jit(solution)/shard_map/dynamic_slice | solution.py:357
  1.5 1.1 %fusion.3 = f32[12]{0:T(128)S(1)} fusion(bf16[12,2,36,16]{2,3,1,0:T(8,128)(2,1)} %param.6, f32[16]{0:T(128)S(1)} %dynamic_slice.3), kind=kLoop, calls=%fused_computation.6 | loop fusion | flops 55284 | bytes 27760 | tf_op jit(solution)/shard_map/reduce_sum | solution.py:367
  2.6 0.1 broadcast_in_dim.2.h_ref
  2.7 0.1 fusion.12
  2.8 0.1 negate_convert_fusion
  2.9 1.1 %fusion.2 = bf16[16,36,2,12]{1,0,3,2:T(8,128)(2,1)S(1)} fusion(bf16[12,2,36,16]{2,3,1,0:T(8,128)(2,1)} %param.6, f32[16]{0:T(128)S(1)} %dynamic_slice.3, bf16[1,36,2,36]{3,1,0,2:T(8,128)(2,1)S(1)} %get-tuple-element.11, bf16[1,36,2,36]{3,1,0,2:T(8,128)(2,1)S(1)} %get-tuple-element.10), kind=kOutput, calls=%fused_computation.3 | convolution fusion | flops 2039040 | bytes 65728 | tf_op jit(solution)/shard_map/cpar,paqm->rmqc/dot_general | solution.py:359
  4.0 0.3 copy.12
  4.4 0.2 reshape.111
  4.6 0.0 copy-done.2
  4.6 0.8 %reshape.117 = bf16[36,64,256]{2,0,1:T(8,128)(2,1)S(1)} reshape(bf16[36,64,2,128]{3,2,0,1:T(2,128)(2,1)S(1)} %bitcast.34) | data formatting | bytes 2359296 | tf_op jit(solution)/shard_map/reshape | solution.py:369
  5.4 0.0 copy-start
  5.4 0.0 copy-start.1
  5.5 0.3 copy.17.x_ref
  5.7 0.6 %copy-done = f32[5,36,256]{2,1,0:T(8,128)S(1)} copy-done((f32[5,36,256]{2,1,0:T(8,128)S(1)}, f32[5,36,256]{2,1,0:T(8,128)}, u32[]{:S(2)}) %copy-start) | copy-done | bytes 184344
  6.4 0.1 copy-done.1
  6.5 37.7 %shard_map.68 = (f32[16,896]{1,0:T(8,128)S(1)}, f32[16,128]{1,0:T(8,128)S(1)}, f32[8,64]{1,0:T(8,128)S(1)}) custom-call(bf16[16,896]{1,0:T(8,128)(2,1)S(1)} %pad.8.w_ref, f32[16,128]{1,0:T(8,128)S(1)} %broadcast_in_dim.2.h_ref, bf16[36,64,256]{2,1,0:T(8,128)(2,1)S(1)} %copy.17.x_ref, f32[5,36,256]{2,1,0:T(8,128)S(1)} %copy-done.1, f32[5,36,256]{2,1,0:T(8,128)S(1)} %copy-done), custom_call_target="tpu_custom_call" | custom-call | tf_op jit(solution)/shard_map/pallas_call | solution.py:331
  44.2 0.1 slice_reduce_fusion
  44.3 0.5 %slice_bitcast_fusion = f32[64]{0:T(128)} fusion(f32[8,64]{1,0:T(8,128)S(1)} %get-tuple-element.7), kind=kLoop, calls=%fused_computation.26 | loop fusion | bytes 512 | tf_op jit(solution)/shard_map/squeeze | solution.py:378
  44.8 0.1 add_divide_fusion
  44.9 0.8 %reshape.113 = f32[16,36,2,12]{3,2,1,0:T(2,128)S(1)} reshape(f32[16,864]{1,0:T(8,128)S(1)} %bitcast.33) | data formatting | bytes 110592 | tf_op jit(solution)/shard_map/reshape | solution.py:374
  45.7 0.2 bitcast_multiply_fusion
  45.9 1.0 %copy.14 = f32[12,2,36,16]{2,3,1,0:T(8,128)} copy(f32[12,2,36,16]{0,1,2,3:T(2,128)S(1)} %bitcast_multiply_fusion) | data formatting | bytes 110592
  (3 shorter events, 0.0 us)
Async XLA Ops:
  0.6 4.0 %copy-start.2 = (bf16[64,2,36,128]{3,1,2,0:T(2,128)(2,1)S(1)}, bf16[64,2,36,128]{3,1,2,0:T(2,128)(2,1)}, u32[]{:S(2)}) copy-start(bf16[64,2,36,128]{3,1,2,0:T(2,128)(2,1)} %param.5) | copy-start | bytes 3538948
  5.4 0.9 %copy-start = (f32[5,36,256]{2,1,0:T(8,128)S(1)}, f32[5,36,256]{2,1,0:T(8,128)}, u32[]{:S(2)}) copy-start(f32[5,36,256]{2,1,0:T(8,128)} %constant.40.clone.s_ref) | copy-start | bytes 552964
  5.4 1.0 %copy-start.1 = (f32[5,36,256]{2,1,0:T(8,128)S(1)}, f32[5,36,256]{2,1,0:T(8,128)}, u32[]{:S(2)}) copy-start(f32[5,36,256]{2,1,0:T(8,128)} %constant.39.clone.c_ref) | copy-start | bytes 552964

commit v4 on v3

--- a/solution.py
+++ b/solution.py
@@ -45,13 +45,13 @@
     pl.semaphore_wait(barrier, sum(counts.values()) - len(counts))
 
 
-def push(axis, count, me, source, land, send_sem, recv_sem):
+def push(axis, count, me, source, land, send_sem, recv_sem, lanes=None):
     copies = []
     for step in range(1, count):
         peer = lax.rem(me + step, count)
         copy = pltpu.make_async_remote_copy(
             src_ref=source(peer),
-            dst_ref=land.at[me],
+            dst_ref=land.at[me] if lanes is None else land.at[me, :, lanes],
             send_sem=send_sem.at[step],
             recv_sem=recv_sem.at[step],
             device_id={axis: peer},
@@ -207,7 +207,7 @@
         )
         return carry
 
-    lax.fori_loop(0, angles, correlate, 0)
+    lax.fori_loop(0, angles, correlate, 0, unroll=6)
 
     def keep_score(k, value):
         scores[k] = value[:padded] * (1.0 / angles) - half_norms
@@ -223,7 +223,9 @@
     def spread(values):
         return jnp.concatenate([values] * SHIFTS, axis=1)
 
-    highest = lax.fori_loop(1, angles, lambda k, best: jnp.maximum(best, scores[k]), scores[0])
+    highest = scores[0]
+    for k in range(1, angles):
+        highest = jnp.maximum(highest, scores[k])
     peak = fold(jnp.max(highest, axis=0, keepdims=True), jnp.maximum)
     wide_peak = spread(peak)
 
@@ -232,7 +234,8 @@
         scores[k] = value
         return total + value
 
-    class_total = lax.fori_loop(0, angles, exponentiate, jnp.zeros(scores.shape[1:], jnp.float32))
+    empty = jnp.zeros(scores.shape[1:], jnp.float32)
+    class_total = lax.fori_loop(0, angles, exponentiate, empty, unroll=6)
     total = fold(jnp.sum(class_total, axis=0, keepdims=True), jnp.add)
     row = lax.broadcasted_iota(jnp.int32, stat.shape, 0)
     stat[...] = jnp.where(row == 0, peak, total)
@@ -276,18 +279,27 @@
         )
         return carry
 
-    lax.fori_loop(0, angles, accumulate, 0)
-    rows = outgoing.shape[1]
-    for block in range(sums.shape[0] // BLOCK):
-        lanes = slice(block * BLOCK, (block + 1) * BLOCK)
-        piece = sums[lanes, :].T
-        for index in range(dom):
-            part = piece[index * cycle_count : (index + 1) * cycle_count]
-            if rows > cycle_count:
-                gap = jnp.zeros((rows - cycle_count, BLOCK), jnp.float32)
-                part = jnp.concatenate([part, gap], axis=0)
-            outgoing[index, :, lanes] = part.astype(outgoing.dtype)
-    copies += push("dom", dom, me, lambda peer: outgoing.at[peer], land, o_send, o_recv)
+    rows, blocks = outgoing.shape[1], sums.shape[0] // BLOCK
+    split = (blocks + 1) // 2
+    ready = min(angles, -(-split * BLOCK // pairs))
+    for part, (first, last, head, tail) in enumerate(
+        ((0, ready, 0, split), (ready, angles, split, blocks))
+    ):
+        lax.fori_loop(first, last, accumulate, 0, unroll=6)
+        for block in range(head, tail):
+            lanes = slice(block * BLOCK, (block + 1) * BLOCK)
+            piece = sums[lanes, :].T
+            for index in range(dom):
+                own = piece[index * cycle_count : (index + 1) * cycle_count]
+                if rows > cycle_count:
+                    gap = jnp.zeros((rows - cycle_count, BLOCK), jnp.float32)
+                    own = jnp.concatenate([own, gap], axis=0)
+                outgoing[index, :, lanes] = own.astype(outgoing.dtype)
+        lanes = slice(head * BLOCK, tail * BLOCK)
+        copies += push(
+            "dom", dom, me, lambda peer: outgoing.at[peer, :, lanes], land,
+            o_send.at[part], o_recv.at[part], lanes,
+        )
     land[me] = outgoing[me]
     for copy in copies:
         copy.wait()
@@ -326,8 +338,8 @@
         pltpu.VMEM((padded, BLOCK), f32),
         pltpu.VMEM((dom, padded, BLOCK), f32),
     ]
-    for count in (dom, dom, cls, dom, dom):
-        scratch += [pltpu.SemaphoreType.DMA((count,))] * 2
+    for shape in ((dom,), (dom,), (cls,), (2, dom), (dom,)):
+        scratch += [pltpu.SemaphoreType.DMA(shape)] * 2
     return pl.pallas_call(
         functools.partial(em_kernel, dom, cls, classes),
         out_shape=(
@@ -353,8 +365,8 @@
     used = classes * 2 * angles
     long = -(-used // BLOCK) * BLOCK
     table = angular_table(angles)
-    cycle_start = lax.axis_index("dom") * cycle_count
-    noise = lax.dynamic_slice_in_dim(noise_weights, cycle_start, cycle_count, 0)
+    mine = jnp.arange(dom)[:, None] == lax.axis_index("dom")
+    noise = jnp.sum(jnp.where(mine, noise_weights.reshape(dom, cycle_count), 0.0), axis=0)
 
     ref_spectra = jnp.einsum(
         "cpar,paqm->rmqc", references, table, preferred_element_type=jnp.float32

time: 47.1 us -> 40.1 us (0.85)
  Pallas kernels: 37.7 us -> 30.6 us
    pallas_call x1, Pallas kernels: 37.7 us -> 30.6 us  [em_step(): pl.pallas_call(functools.partial(em_kernel, dom, cls, classes), out_shape...]
    reshape x0 -> x1, local copies, waits for them, and re-layouts: none -> 0.83 us  [per_device(): noise_weights.reshape(dom, cycle_count)]
    dynamic_slice x1 -> x0, local copies, waits for them, and re-layouts: 0.83 us -> none  [per_device(): noise = lax.dynamic_slice_in_dim(noise_weights, cycle_start, cycle_count, 0)]
where the time goes in v4:
time: 40.1 us; the launch traced here: 39.9 us
  Pallas kernels  30.6 us (76%)
  local copies, waits for them, and re-layouts  5.72 us (14%)
  other arithmetic  1.75 us (4%)
  matrix products  1.11 us (3%)
  between operations  0.75 us (2%)
    pallas_call x1, Pallas kernels, em_step(): pl.pallas_call(functools.partial(em_kernel, dom, cls, classes), out_shape...  30.6 us
    unnamed x7, local copies, waits for them, and re-layouts  1.77 us
    reduce_sum x1, other arithmetic, per_device(): norms = jnp.sum(noise * own_wide * own_wide, axis=(1, 2, 3))  1.13 us
    dot_general x1, matrix products, per_device(): jnp.einsum('cpar,paqm->rmqc', references, table, preferred_element_type=j...  1.11 us
    reshape x2, local copies, waits for them, and re-layouts, per_device(): jnp.transpose(particles, (2, 0, 1, 3))  1.07 us
    reshape x1, local copies, waits for them, and re-layouts, per_device(): noise_weights.reshape(dom, cycle_count)  0.83 us

profile of v4, /device:TPU:0, one launch (start us, length us, event | category | flops | bytes accessed | tf_op | source)
XLA Modules:
  0.0 39.9 jit_solution(7275938587829216742)
XLA Ops:
  0.6 0.0 copy-start.2
  0.7 0.8 %reshape.119 = f32[8,16]{1,0:T(8,128)S(1)} reshape(f32[128]{0:T(128)} %param.7) | data formatting | bytes 1024 | tf_op jit(solution)/shard_map/reshape | solution.py:369
  1.5 0.1 select_reduce_fusion
  1.6 1.1 %fusion.3 = f32[12]{0:T(128)S(1)} fusion(bf16[12,2,36,16]{2,3,1,0:T(8,128)(2,1)} %param.6, f32[16]{0:T(128)S(1)} %select_reduce_fusion), kind=kLoop, calls=%fused_computation.6 | loop fusion | flops 55284 | bytes 27760 | tf_op jit(solution)/shard_map/reduce_sum | solution.py:379
  2.7 0.1 broadcast_in_dim.16.h_ref
  2.8 0.1 fusion.12
  2.9 0.1 negate_convert_fusion
  3.0 1.1 %fusion.2 = bf16[16,36,2,12]{1,0,3,2:T(8,128)(2,1)S(1)} fusion(bf16[12,2,36,16]{2,3,1,0:T(8,128)(2,1)} %param.6, f32[16]{0:T(128)S(1)} %select_reduce_fusion, bf16[1,36,2,36]{3,1,0,2:T(8,128)(2,1)S(1)} %get-tuple-element.11, bf16[1,36,2,36]{3,1,0,2:T(8,128)(2,1)S(1)} %get-tuple-element.10), kind=kOutput, calls=%fused_computation.3 | convolution fusion | flops 2039040 | bytes 65728 | tf_op jit(solution)/shard_map/cpar,paqm->rmqc/dot_general | solution.py:371
  4.1 0.3 copy.12
  4.5 0.2 reshape.120
  4.7 0.0 copy-done.2
  4.7 0.8 %reshape.126 = bf16[36,64,256]{2,0,1:T(8,128)(2,1)S(1)} reshape(bf16[36,64,2,128]{3,2,0,1:T(2,128)(2,1)S(1)} %bitcast.34) | data formatting | bytes 2359296 | tf_op jit(solution)/shard_map/reshape | solution.py:381
  5.5 0.0 copy-start
  5.5 0.0 copy-start.1
  5.6 0.3 copy.17.x_ref
  5.8 0.6 %copy-done = f32[5,36,256]{2,1,0:T(8,128)S(1)} copy-done((f32[5,36,256]{2,1,0:T(8,128)S(1)}, f32[5,36,256]{2,1,0:T(8,128)}, u32[]{:S(2)}) %copy-start) | copy-done | bytes 184344
  6.5 0.1 copy-done.1
  6.6 30.6 %shard_map.68 = (f32[16,896]{1,0:T(8,128)S(1)}, f32[16,128]{1,0:T(8,128)S(1)}, f32[8,64]{1,0:T(8,128)S(1)}) custom-call(bf16[16,896]{1,0:T(8,128)(2,1)S(1)} %pad.8.w_ref, f32[16,128]{1,0:T(8,128)S(1)} %broadcast_in_dim.16.h_ref, bf16[36,64,256]{2,1,0:T(8,128)(2,1)S(1)} %copy.17.x_ref, f32[5,36,256]{2,1,0:T(8,128)S(1)} %copy-done.1, f32[5,36,256]{2,1,0:T(8,128)S(1)} %copy-done), custom_call_target="tpu_custom_call" | custom-call | tf_op jit(solution)/shard_map/pallas_call | solution.py:343
  37.2 0.1 slice_reduce_fusion
  37.3 0.5 %slice_bitcast_fusion = f32[64]{0:T(128)} fusion(f32[8,64]{1,0:T(8,128)S(1)} %get-tuple-element.7), kind=kLoop, calls=%fused_computation.27 | loop fusion | bytes 512 | tf_op jit(solution)/shard_map/squeeze | solution.py:390
  37.8 0.1 add_divide_fusion
  37.9 0.8 %reshape.122 = f32[16,36,2,12]{3,2,1,0:T(2,128)S(1)} reshape(f32[16,864]{1,0:T(8,128)S(1)} %bitcast.33) | data formatting | bytes 110592 | tf_op jit(solution)/shard_map/reshape | solution.py:386
  38.7 0.2 bitcast_multiply_fusion
  38.9 1.0 %copy.14 = f32[12,2,36,16]{2,3,1,0:T(8,128)} copy(f32[12,2,36,16]{0,1,2,3:T(2,128)S(1)} %bitcast_multiply_fusion) | data formatting | bytes 110592
  (4 shorter events, 0.0 us)
Async XLA Ops:
  0.6 4.1 %copy-start.2 = (bf16[64,2,36,128]{3,1,2,0:T(2,128)(2,1)S(1)}, bf16[64,2,36,128]{3,1,2,0:T(2,128)(2,1)}, u32[]{:S(2)}) copy-start(bf16[64,2,36,128]{3,1,2,0:T(2,128)(2,1)} %param.5) | copy-start | bytes 3538948
  5.5 0.9 %copy-start = (f32[5,36,256]{2,1,0:T(8,128)S(1)}, f32[5,36,256]{2,1,0:T(8,128)}, u32[]{:S(2)}) copy-start(f32[5,36,256]{2,1,0:T(8,128)} %constant.36.clone.s_ref) | copy-start | bytes 552964
  5.5 1.0 %copy-start.1 = (f32[5,36,256]{2,1,0:T(8,128)S(1)}, f32[5,36,256]{2,1,0:T(8,128)}, u32[]{:S(2)}) copy-start(f32[5,36,256]{2,1,0:T(8,128)} %constant.35.clone.c_ref) | copy-start | bytes 552964

commit v5 on v4

--- a/solution.py
+++ b/solution.py
@@ -124,13 +124,46 @@
         for part in even:
             total = total + part
         store((odd * quarter * first) % angles, total)
+        products = {}
+
+        def scaled(kind, parts, j, factor):
+            if (kind, j, factor) not in products:
+                products[kind, j, factor] = factor * parts[j - 1]
+            return products[kind, j, factor]
+
+        def weigh(kind, parts, terms):
+            groups = {}
+            for j, factor, sign in terms:
+                groups.setdefault(factor, []).append((j, sign))
+            total = None
+            for factor, members in groups.items():
+                if factor == 0.0:
+                    continue
+                if len(members) == 1:
+                    j, sign = members[0]
+                    part = parts[j - 1] if factor == 1.0 else scaled(kind, parts, j, factor)
+                else:
+                    j, sign = members[0]
+                    part = parts[j - 1]
+                    for other, turn in members[1:]:
+                        value = parts[other - 1]
+                        part = part + value if turn == sign else part - value
+                    part = factor * part
+                if total is None:
+                    total = part if sign > 0 else -part
+                else:
+                    total = total + part if sign > 0 else total - part
+            return total
+
         for k in range(1, pairs + 1):
-            real, imag = head, None
+            cosines, sines = [], []
             for j in range(1, pairs + 1):
-                cosine, sine = root(k * j, odd)
-                real = real + cosine * even[j - 1]
-                term = sine * uneven[j - 1]
-                imag = term if imag is None else imag + term
+                place = (k * j) % odd
+                cosine, sine = root(min(place, odd - place), odd)
+                cosines.append((j, abs(cosine), 1 if cosine >= 0.0 else -1))
+                sines.append((j, sine, 1 if place <= pairs else -1))
+            real = head + weigh("even", even, cosines)
+            imag = weigh("uneven", uneven, sines)
             base = odd * quarter * first
             store((base + 4 * inverse * k) % angles, real + imag)
             store((base + 4 * inverse * (odd - k)) % angles, real - imag)
@@ -209,10 +242,18 @@
 
     lax.fori_loop(0, angles, correlate, 0, unroll=6)
 
-    def keep_score(k, value):
-        scores[k] = value[:padded] * (1.0 / angles) - half_norms
-
-    transform(lambda m: corr[m], wide_middle, keep_score, angles, full_root, 0)
+    images = SHIFTS * particle_count
+    pieces = [slice(start, min(start + BLOCK, images)) for start in range(0, images, BLOCK)]
+
+    def score_piece(lanes):
+        def keep_score(k, value):
+            scores[k, :, lanes] = value[:padded] * (1.0 / angles) - half_norms
+
+        middle_piece = wide_middle.at[:, :, :, lanes]
+        transform(lambda m: corr[m, :, lanes], middle_piece, keep_score, angles, full_root, 0)
+
+    for lanes in pieces:
+        score_piece(lanes)
 
     def fold(values, combine):
         parts = [
@@ -257,14 +298,20 @@
     copies = push("dom", dom, me, lambda peer: total_block, total_land, t_send, t_recv)
     total_land[me] = total_block[...]
 
-    def load_posterior(k):
-        value = scores[k] * scale
-        return jnp.concatenate([value, jnp.zeros_like(value)], axis=0)
-
-    def keep_weight(m, value):
-        weights[m] = jnp.concatenate([value[:padded], -value[padded:]], axis=0).astype(weights.dtype)
-
-    transform(load_posterior, wide_middle, keep_weight, angles, full_root, 0)
+    def weight_piece(lanes):
+        def load_posterior(k):
+            value = scores[k, :, lanes] * scale[:, lanes]
+            return jnp.concatenate([value, jnp.zeros_like(value)], axis=0)
+
+        def keep_weight(m, value):
+            both = jnp.concatenate([value[:padded], -value[padded:]], axis=0)
+            weights[m, :, lanes] = both.astype(weights.dtype)
+
+        middle_piece = wide_middle.at[:, :, :, lanes]
+        transform(load_posterior, middle_piece, keep_weight, angles, full_root, 0)
+
+    for lanes in pieces:
+        weight_piece(lanes)
 
     used = angles * pairs
     if sums.shape[0] > used:

time: 40.1 us -> 40 us (level)
  no operation moved by 1% of the time
where the time goes in v5:
time: 40 us; the launch traced here: 39.8 us
  Pallas kernels  30.5 us (76%)
  local copies, waits for them, and re-layouts  5.72 us (14%)
  other arithmetic  1.75 us (4%)
  matrix products  1.11 us (3%)
  between operations  0.75 us (2%)
    pallas_call x1, Pallas kernels, em_step(): pl.pallas_call(functools.partial(em_kernel, dom, cls, classes), out_shape...  30.5 us
    unnamed x7, local copies, waits for them, and re-layouts  1.77 us
    reduce_sum x1, other arithmetic, per_device(): norms = jnp.sum(noise * own_wide * own_wide, axis=(1, 2, 3))  1.13 us
    dot_general x1, matrix products, per_device(): jnp.einsum('cpar,paqm->rmqc', references, table, preferred_element_type=j...  1.11 us
    reshape x2, local copies, waits for them, and re-layouts, per_device(): jnp.transpose(particles, (2, 0, 1, 3))  1.07 us
    reshape x1, local copies, waits for them, and re-layouts, per_device(): noise_weights.reshape(dom, cycle_count)  0.83 us

profile of v5, /device:TPU:0, one launch (start us, length us, event | category | flops | bytes accessed | tf_op | source)
XLA Modules:
  0.0 39.8 jit_solution(12052046249330062653)
XLA Ops:
  0.6 0.0 copy-start.2
  0.7 0.8 %reshape.119 = f32[8,16]{1,0:T(8,128)S(1)} reshape(f32[128]{0:T(128)} %param.7) | data formatting | bytes 1024 | tf_op jit(solution)/shard_map/reshape | solution.py:416
  1.5 0.1 select_reduce_fusion
  1.6 1.1 %fusion.3 = f32[12]{0:T(128)S(1)} fusion(bf16[12,2,36,16]{2,3,1,0:T(8,128)(2,1)} %param.6, f32[16]{0:T(128)S(1)} %select_reduce_fusion), kind=kLoop, calls=%fused_computation.6 | loop fusion | flops 55284 | bytes 27760 | tf_op jit(solution)/shard_map/reduce_sum | solution.py:426
  2.7 0.1 broadcast_in_dim.16.h_ref
  2.8 0.1 fusion.12
  2.9 0.1 negate_convert_fusion
  3.0 1.1 %fusion.2 = bf16[16,36,2,12]{1,0,3,2:T(8,128)(2,1)S(1)} fusion(bf16[12,2,36,16]{2,3,1,0:T(8,128)(2,1)} %param.6, f32[16]{0:T(128)S(1)} %select_reduce_fusion, bf16[1,36,2,36]{3,1,0,2:T(8,128)(2,1)S(1)} %get-tuple-element.11, bf16[1,36,2,36]{3,1,0,2:T(8,128)(2,1)S(1)} %get-tuple-element.10), kind=kOutput, calls=%fused_computation.3 | convolution fusion | flops 2039040 | bytes 65728 | tf_op jit(solution)/shard_map/cpar,paqm->rmqc/dot_general | solution.py:418
  4.1 0.3 copy.12
  4.5 0.2 reshape.120
  4.7 0.0 copy-done.2
  4.7 0.8 %reshape.126 = bf16[36,64,256]{2,0,1:T(8,128)(2,1)S(1)} reshape(bf16[36,64,2,128]{3,2,0,1:T(2,128)(2,1)S(1)} %bitcast.34) | data formatting | bytes 2359296 | tf_op jit(solution)/shard_map/reshape | solution.py:428
  5.5 0.0 copy-start
  5.5 0.0 copy-start.1
  5.6 0.3 copy.17.x_ref
  5.8 0.6 %copy-done = f32[5,36,256]{2,1,0:T(8,128)S(1)} copy-done((f32[5,36,256]{2,1,0:T(8,128)S(1)}, f32[5,36,256]{2,1,0:T(8,128)}, u32[]{:S(2)}) %copy-start) | copy-done | bytes 184344
  6.5 0.1 copy-done.1
  6.6 30.5 %shard_map.68 = (f32[16,896]{1,0:T(8,128)S(1)}, f32[16,128]{1,0:T(8,128)S(1)}, f32[8,64]{1,0:T(8,128)S(1)}) custom-call(bf16[16,896]{1,0:T(8,128)(2,1)S(1)} %pad.8.w_ref, f32[16,128]{1,0:T(8,128)S(1)} %broadcast_in_dim.16.h_ref, bf16[36,64,256]{2,1,0:T(8,128)(2,1)S(1)} %copy.17.x_ref, f32[5,36,256]{2,1,0:T(8,128)S(1)} %copy-done.1, f32[5,36,256]{2,1,0:T(8,128)S(1)} %copy-done), custom_call_target="tpu_custom_call" | custom-call | tf_op jit(solution)/shard_map/pallas_call | solution.py:390
  37.1 0.1 slice_reduce_fusion
  37.2 0.5 %slice_bitcast_fusion = f32[64]{0:T(128)} fusion(f32[8,64]{1,0:T(8,128)S(1)} %get-tuple-element.7), kind=kLoop, calls=%fused_computation.27 | loop fusion | bytes 512 | tf_op jit(solution)/shard_map/squeeze | solution.py:437
  37.7 0.1 add_divide_fusion
  37.8 0.8 %reshape.122 = f32[16,36,2,12]{3,2,1,0:T(2,128)S(1)} reshape(f32[16,864]{1,0:T(8,128)S(1)} %bitcast.33) | data formatting | bytes 110592 | tf_op jit(solution)/shard_map/reshape | solution.py:433
  38.6 0.2 bitcast_multiply_fusion
  38.8 1.0 %copy.14 = f32[12,2,36,16]{2,3,1,0:T(8,128)} copy(f32[12,2,36,16]{0,1,2,3:T(2,128)S(1)} %bitcast_multiply_fusion) | data formatting | bytes 110592
  (4 shorter events, 0.0 us)
Async XLA Ops:
  0.6 4.1 %copy-start.2 = (bf16[64,2,36,128]{3,1,2,0:T(2,128)(2,1)S(1)}, bf16[64,2,36,128]{3,1,2,0:T(2,128)(2,1)}, u32[]{:S(2)}) copy-start(bf16[64,2,36,128]{3,1,2,0:T(2,128)(2,1)} %param.5) | copy-start | bytes 3538948
  5.5 0.9 %copy-start = (f32[5,36,256]{2,1,0:T(8,128)S(1)}, f32[5,36,256]{2,1,0:T(8,128)}, u32[]{:S(2)}) copy-start(f32[5,36,256]{2,1,0:T(8,128)} %constant.36.clone.s_ref) | copy-start | bytes 552964
  5.5 1.0 %copy-start.1 = (f32[5,36,256]{2,1,0:T(8,128)S(1)}, f32[5,36,256]{2,1,0:T(8,128)}, u32[]{:S(2)}) copy-start(f32[5,36,256]{2,1,0:T(8,128)} %constant.35.clone.c_ref) | copy-start | bytes 552964

commit v6 on v4

--- a/solution.py
+++ b/solution.py
@@ -207,7 +207,7 @@
         )
         return carry
 
-    lax.fori_loop(0, angles, correlate, 0, unroll=6)
+    lax.fori_loop(0, angles, correlate, 0, unroll=12)
 
     def keep_score(k, value):
         scores[k] = value[:padded] * (1.0 / angles) - half_norms
@@ -285,7 +285,7 @@
     for part, (first, last, head, tail) in enumerate(
         ((0, ready, 0, split), (ready, angles, split, blocks))
     ):
-        lax.fori_loop(first, last, accumulate, 0, unroll=6)
+        lax.fori_loop(first, last, accumulate, 0, unroll=12)
         for block in range(head, tail):
             lanes = slice(block * BLOCK, (block + 1) * BLOCK)
             piece = sums[lanes, :].T

time: 40.1 us -> 40.1 us (level)
  no operation moved by 1% of the time
where the time goes in v6:
time: 40.1 us; the launch traced here: 39.9 us
  Pallas kernels  30.5 us (76%)
  local copies, waits for them, and re-layouts  5.72 us (14%)
  other arithmetic  1.75 us (4%)
  matrix products  1.11 us (3%)
  between operations  0.75 us (2%)
    pallas_call x1, Pallas kernels, em_step(): pl.pallas_call(functools.partial(em_kernel, dom, cls, classes), out_shape...  30.5 us
    unnamed x7, local copies, waits for them, and re-layouts  1.77 us
    reduce_sum x1, other arithmetic, per_device(): norms = jnp.sum(noise * own_wide * own_wide, axis=(1, 2, 3))  1.13 us
    dot_general x1, matrix products, per_device(): jnp.einsum('cpar,paqm->rmqc', references, table, preferred_element_type=j...  1.11 us
    reshape x2, local copies, waits for them, and re-layouts, per_device(): jnp.transpose(particles, (2, 0, 1, 3))  1.07 us
    reshape x1, local copies, waits for them, and re-layouts, per_device(): noise_weights.reshape(dom, cycle_count)  0.83 us

profile of v6, /device:TPU:0, one launch (start us, length us, event | category | flops | bytes accessed | tf_op | source)
XLA Modules:
  0.0 39.9 jit_solution(17006891474002178228)
XLA Ops:
  0.6 0.0 copy-start.2
  0.7 0.8 %reshape.119 = f32[8,16]{1,0:T(8,128)S(1)} reshape(f32[128]{0:T(128)} %param.7) | data formatting | bytes 1024 | tf_op jit(solution)/shard_map/reshape | solution.py:369
  1.5 0.1 select_reduce_fusion
  1.6 1.1 %fusion.3 = f32[12]{0:T(128)S(1)} fusion(bf16[12,2,36,16]{2,3,1,0:T(8,128)(2,1)} %param.6, f32[16]{0:T(128)S(1)} %select_reduce_fusion), kind=kLoop, calls=%fused_computation.6 | loop fusion | flops 55284 | bytes 27760 | tf_op jit(solution)/shard_map/reduce_sum | solution.py:379
  2.7 0.1 broadcast_in_dim.16.h_ref
  2.8 0.1 fusion.12
  2.9 0.1 negate_convert_fusion
  3.0 1.1 %fusion.2 = bf16[16,36,2,12]{1,0,3,2:T(8,128)(2,1)S(1)} fusion(bf16[12,2,36,16]{2,3,1,0:T(8,128)(2,1)} %param.6, f32[16]{0:T(128)S(1)} %select_reduce_fusion, bf16[1,36,2,36]{3,1,0,2:T(8,128)(2,1)S(1)} %get-tuple-element.11, bf16[1,36,2,36]{3,1,0,2:T(8,128)(2,1)S(1)} %get-tuple-element.10), kind=kOutput, calls=%fused_computation.3 | convolution fusion | flops 2039040 | bytes 65728 | tf_op jit(solution)/shard_map/cpar,paqm->rmqc/dot_general | solution.py:371
  4.1 0.3 copy.12
  4.5 0.2 reshape.120
  4.7 0.0 copy-done.2
  4.7 0.8 %reshape.126 = bf16[36,64,256]{2,0,1:T(8,128)(2,1)S(1)} reshape(bf16[36,64,2,128]{3,2,0,1:T(2,128)(2,1)S(1)} %bitcast.34) | data formatting | bytes 2359296 | tf_op jit(solution)/shard_map/reshape | solution.py:381
  5.5 0.0 copy-start
  5.5 0.0 copy-start.1
  5.6 0.3 copy.17.x_ref
  5.8 0.6 %copy-done = f32[5,36,256]{2,1,0:T(8,128)S(1)} copy-done((f32[5,36,256]{2,1,0:T(8,128)S(1)}, f32[5,36,256]{2,1,0:T(8,128)}, u32[]{:S(2)}) %copy-start) | copy-done | bytes 184344
  6.5 0.1 copy-done.1
  6.6 30.5 %shard_map.68 = (f32[16,896]{1,0:T(8,128)S(1)}, f32[16,128]{1,0:T(8,128)S(1)}, f32[8,64]{1,0:T(8,128)S(1)}) custom-call(bf16[16,896]{1,0:T(8,128)(2,1)S(1)} %pad.8.w_ref, f32[16,128]{1,0:T(8,128)S(1)} %broadcast_in_dim.16.h_ref, bf16[36,64,256]{2,1,0:T(8,128)(2,1)S(1)} %copy.17.x_ref, f32[5,36,256]{2,1,0:T(8,128)S(1)} %copy-done.1, f32[5,36,256]{2,1,0:T(8,128)S(1)} %copy-done), custom_call_target="tpu_custom_call" | custom-call | tf_op jit(solution)/shard_map/pallas_call | solution.py:343
  37.1 0.1 slice_reduce_fusion
  37.2 0.5 %slice_bitcast_fusion = f32[64]{0:T(128)} fusion(f32[8,64]{1,0:T(8,128)S(1)} %get-tuple-element.7), kind=kLoop, calls=%fused_computation.27 | loop fusion | bytes 512 | tf_op jit(solution)/shard_map/squeeze | solution.py:390
  37.8 0.1 add_divide_fusion
  37.8 0.8 %reshape.122 = f32[16,36,2,12]{3,2,1,0:T(2,128)S(1)} reshape(f32[16,864]{1,0:T(8,128)S(1)} %bitcast.33) | data formatting | bytes 110592 | tf_op jit(solution)/shard_map/reshape | solution.py:386
  38.6 0.2 bitcast_multiply_fusion
  38.9 1.0 %copy.14 = f32[12,2,36,16]{2,3,1,0:T(8,128)} copy(f32[12,2,36,16]{0,1,2,3:T(2,128)S(1)} %bitcast_multiply_fusion) | data formatting | bytes 110592
  (4 shorter events, 0.0 us)
Async XLA Ops:
  0.6 4.1 %copy-start.2 = (bf16[64,2,36,128]{3,1,2,0:T(2,128)(2,1)S(1)}, bf16[64,2,36,128]{3,1,2,0:T(2,128)(2,1)}, u32[]{:S(2)}) copy-start(bf16[64,2,36,128]{3,1,2,0:T(2,128)(2,1)} %param.5) | copy-start | bytes 3538948
  5.5 0.9 %copy-start = (f32[5,36,256]{2,1,0:T(8,128)S(1)}, f32[5,36,256]{2,1,0:T(8,128)}, u32[]{:S(2)}) copy-start(f32[5,36,256]{2,1,0:T(8,128)} %constant.36.clone.s_ref) | copy-start | bytes 552964
  5.5 1.0 %copy-start.1 = (f32[5,36,256]{2,1,0:T(8,128)S(1)}, f32[5,36,256]{2,1,0:T(8,128)}, u32[]{:S(2)}) copy-start(f32[5,36,256]{2,1,0:T(8,128)} %constant.35.clone.c_ref) | copy-start | bytes 552964
